TPU v7x, 32 devices: a whole 2x2x4 slice. The times are simulated.
32 devices in a mesh: groups: 2 (over x), elec: 16 (over z, y, core).
Axes of the slice: x: 2, y: 2, z: 4, core: 2. Of those that a mesh axis runs over, the one named last changes fastest.
Arguments:
- features: bfloat16 [131072, 256], P(('groups', 'elec')), parts along dimension 0, may hold values from -6 to 6
- assignment: int32 [131072], P(('groups', 'elec')), parts along dimension 0, may hold values from 0 to 65535, as said below
- pairs: int32 [2048, 3], P(('groups', 'elec')), parts along dimension 0, may hold values from 0 to 1023, as said below
- w_query: bfloat16 [256, 256], replicated
- w_key: bfloat16 [256, 256], replicated
- w_value: bfloat16 [256, 256], replicated, may hold values from -0.375 to 0.375
- w_out: bfloat16 [256, 256], replicated, may hold values from -0.375 to 0.375
- w_mix: bfloat16 [256, 256], replicated, may hold values from -0.375 to 0.375
Outputs:
- mixed: bfloat16 [131072, 256], P(('groups', 'elec')), parts along dimension 0
There are 2 independent parts, one for each index of `groups`. A program takes and returns all parts, laid end to end along the dimension named above; an argument that names none is the same for every part. Nothing has to cross between parts.
Inputs may be any that keep to these rules, and one draw needn't show every extreme that they name: assignment is a permutation of the rows; each group of 512 rows of one walker on one device is filled from electrons of that same group. pairs[b, :] name blocks of block b's own walker (its blocks lie on the 8 devices whose index has the same remainder modulo 1024 // 512 as block b's device, 8 on each). Over the 64 reader blocks of one device, at most 25 of the listed key blocks lie on any one device (blocks d * 64 to (d + 1) * 64 - 1 lie on device d), and exactly 25 on some device.
All inputs are finite; a program needn't handle non-finite values.
Results may differ from a plain program's by a relative error of at most 0.0078.
Values may be sent and summed in bfloat16 or wider, within the bound.
A program may use at most 128 MiB of HBM per device.

v0:
```python
import functools
import math

import jax
import jax.numpy as jnp
from jax import lax
from jax.experimental import pallas as pl
from jax.experimental.pallas import tpu as pltpu
from jax.sharding import PartitionSpec as P

HEADS = 16
SPAN = 8
LANES = 128
MESH = pl.DeviceIdType.MESH


def layer_norm(rows):
    mean = jnp.mean(rows, axis=-1, keepdims=True)
    centred = rows - mean
    variance = jnp.mean(centred * centred, axis=-1, keepdims=True)
    return centred * lax.rsqrt(variance + 1e-05)


def slot_table(listed, block_count, capacity, position, stride):
    flattened = listed.reshape(-1)
    owner_device = flattened // block_count
    within = flattened % block_count
    entries = flattened.shape[0]
    offset = (position - owner_device // stride) % SPAN
    alike = offset[:, None] == offset[None, :]
    earlier = jnp.arange(entries)[None, :] < jnp.arange(entries)[:, None]
    ranking = jnp.sum(jnp.where(alike & earlier, 1, 0), axis=1).astype(jnp.int32)
    slots = offset * capacity + ranking
    columns = jnp.arange(SPAN * LANES, dtype=jnp.int32)
    matches = (offset * LANES + ranking)[None, :] == columns[:, None]
    tables = jnp.sum(jnp.where(matches, within[None, :], 0), axis=1)
    return slots, tables.astype(jnp.int32).reshape(SPAN, 1, LANES)


def place_kernel(local_ref, features_ref, placed_ref, normed_ref):
    groups, _, size = local_ref.shape
    lane = lax.broadcasted_iota(jnp.int32, (size, LANES), 1).astype(jnp.float32)
    for i in range(groups):
        rows = pl.ds(i * size, size)
        takes = jnp.broadcast_to(local_ref[i].astype(jnp.float32), (LANES, size)).T
        one_hot = jnp.concatenate(
            [jnp.where(takes == lane + k, 1.0, 0.0) for k in range(0, size, LANES)], axis=1
        ).astype(jnp.bfloat16)
        placed = jnp.dot(one_hot, features_ref[rows, :], preferred_element_type=jnp.float32)
        placed_ref[rows, :] = placed.astype(jnp.bfloat16)
        normed_ref[rows, :] = layer_norm(placed).astype(jnp.bfloat16)


def exchange_kernel(
    capacity, stride, blocks_ref, tables_ref, arrived_ref,
    wanted, wanted_s, outbox, t_send, t_recv, d_send, d_recv, local_sem,
):
    me = lax.axis_index("elec")
    group = lax.axis_index("groups")
    peers = lax.axis_size("elec")
    cluster = blocks_ref.shape[1]

    def toward(step):
        return (group, lax.rem(me + step * stride + peers, peers))

    barrier = pltpu.get_barrier_semaphore()
    for step in range(1, SPAN):
        pl.semaphore_signal(barrier, inc=1, device_id=toward(step), device_id_type=MESH)
    pl.semaphore_wait(barrier, SPAN - 1)

    order = sorted(range(1, SPAN), key=lambda s: abs(s - SPAN // 2))
    asks = {}
    for step in order:
        asks[step] = pltpu.make_async_remote_copy(
            src_ref=tables_ref.at[step], dst_ref=wanted.at[step],
            send_sem=t_send.at[step], recv_sem=t_recv.at[step],
            device_id=toward(-step), device_id_type=MESH,
        )
        asks[step].start()

    def gather(step, source):
        copy = pltpu.make_async_copy(source, wanted_s.at[step], local_sem.at[step])
        copy.start()
        copy.wait()

        def one(k, carry):
            start = pl.multiple_of(k * cluster, cluster)
            outbox[step, pl.ds(start, cluster), :] = blocks_ref[wanted_s[step, 0, k]]
            return carry

        lax.fori_loop(0, capacity, one, 0)

    sends = []
    for step in order:
        asks[step].wait_recv()
        gather(step, wanted.at[step])
        send = pltpu.make_async_remote_copy(
            src_ref=outbox.at[step], dst_ref=arrived_ref.at[step],
            send_sem=d_send.at[step], recv_sem=d_recv.at[step],
            device_id=toward(step), device_id_type=MESH,
        )
        send.start()
        sends.append(send)
    gather(0, tables_ref.at[0])
    own = pltpu.make_async_copy(outbox.at[0], arrived_ref.at[0], local_sem.at[SPAN])
    own.start()
    for step in order:
        asks[step].wait_send()
    own.wait()
    for send in sends:
        send.wait()


def attend_kernel(
    slots_ref, placed_ref, normed_ref, arrived_ref, wq_ref, wk_ref, wv_ref, wo_ref, wm_ref,
    out_ref, queries, attended,
):
    cluster, width = arrived_ref.shape[1:]
    rows = placed_ref.shape[0]
    blocks = rows // cluster
    pair_count = slots_ref.shape[0] // (blocks * pl.num_programs(0))
    head_width = width // HEADS
    half = LANES // 2
    per = half // head_width
    first = pl.program_id(0) * blocks
    f32, bf16 = jnp.float32, jnp.bfloat16
    lane = lax.broadcasted_iota(jnp.int32, (cluster, LANES), 1)
    low = lane < half
    low_keys = lax.broadcasted_iota(jnp.int32, ((pair_count + 1) * cluster, LANES), 1) < half
    chosen = [jnp.where(lane // head_width == c, 1.0, 0.0).astype(bf16) for c in range(2 * per)]
    own_head = lane % half // head_width
    scale = math.log2(math.e) / head_width**0.5
    queries[...] = (
        jnp.dot(normed_ref[...], wq_ref[...], preferred_element_type=f32) * scale
    ).astype(bf16)

    def one(j, carry):
        start = pl.multiple_of(j * cluster, cluster)
        base = (first + j) * pair_count
        listed = [arrived_ref[slots_ref[base + p]] for p in range(pair_count)]
        key_rows = jnp.concatenate([normed_ref[pl.ds(start, cluster), :]] + listed, axis=0)
        keys = jnp.dot(key_rows, wk_ref[...], preferred_element_type=f32).astype(bf16)
        values = jnp.dot(key_rows, wv_ref[...], preferred_element_type=f32)
        for band in range(0, width, LANES):
            query = queries[pl.ds(start, cluster), band : band + LANES]
            band_keys = keys[:, band : band + LANES]
            band_values = values[:, band : band + LANES]
            folded = []
            for side in range(2):
                stacked = jnp.concatenate(
                    [query * chosen[side * per + c] for c in range(per)], axis=0
                )
                scores = lax.dot_general(
                    stacked, band_keys, (((1,), (1,)), ((), ())), preferred_element_type=f32
                )
                weights = jnp.exp2(scores - jnp.max(scores, axis=1, keepdims=True)).astype(bf16)
                with_ones = (
                    jnp.where(low_keys, band_values, 1.0)
                    if side == 0
                    else jnp.where(low_keys, 1.0, band_values)
                ).astype(bf16)
                result = jnp.dot(weights, with_ones, preferred_element_type=f32)
                kept = result[(per - 1) * cluster :]
                for c in range(per - 1):
                    kept = jnp.where(own_head == c, result[c * cluster : (c + 1) * cluster], kept)
                folded.append(kept)
            numerator = jnp.where(low, folded[0], folded[1])
            denominator = pltpu.roll(jnp.where(low, folded[1], folded[0]), half, 1)
            attended[pl.ds(start, cluster), band : band + LANES] = (
                numerator / denominator
            ).astype(bf16)
        return carry

    lax.fori_loop(0, blocks, one, 0, unroll=True)
    projected = jnp.dot(attended[...], wo_ref[...], preferred_element_type=f32)
    middle = (placed_ref[...].astype(f32) + projected).astype(bf16).astype(f32)
    second = layer_norm(middle).astype(bf16)
    mixed = middle + jnp.tanh(jnp.dot(second, wm_ref[...], preferred_element_type=f32))
    out_ref[...] = mixed.astype(bf16)


def body(features, assignment, pairs, w_query, w_key, w_value, w_out, w_mix):
    rows_dev, width = features.shape
    block_count, pair_count = pairs.shape
    cluster = rows_dev // block_count
    capacity = (block_count * pair_count + SPAN - 1) // SPAN + 1
    stride = lax.axis_size("elec") // SPAN
    device_index = lax.axis_index("elec")
    position = device_index // stride
    group_rows = SPAN * cluster
    groups = rows_dev // group_rows
    bf16 = jnp.bfloat16

    local = (assignment - device_index * rows_dev).reshape(groups, 1, group_rows)
    local = local - group_rows * jnp.arange(groups, dtype=jnp.int32)[:, None, None]
    batch = math.gcd(groups, 2)
    tile = pl.BlockSpec((batch * group_rows, width), lambda i: (i, 0))
    placed, normed = pl.pallas_call(
        place_kernel,
        grid=(groups // batch,),
        in_specs=[pl.BlockSpec((batch, 1, group_rows), lambda i: (i, 0, 0)), tile],
        out_specs=[tile, tile],
        out_shape=[jax.ShapeDtypeStruct((rows_dev, width), bf16)] * 2,
    )(local, features)

    slots, tables = slot_table(pairs, block_count, capacity, position, stride)
    arrived = pl.pallas_call(
        functools.partial(exchange_kernel, capacity, stride),
        in_specs=[pl.BlockSpec(memory_space=pltpu.VMEM)] * 2,
        out_specs=pl.BlockSpec(memory_space=pl.ANY),
        out_shape=jax.ShapeDtypeStruct((SPAN, capacity * cluster, width), bf16),
        scratch_shapes=[
            pltpu.VMEM((SPAN, 1, LANES), jnp.int32),
            pltpu.SMEM((SPAN, 1, LANES), jnp.int32),
            pltpu.VMEM((SPAN, capacity * cluster, width), bf16),
            pltpu.SemaphoreType.DMA((SPAN,)),
            pltpu.SemaphoreType.DMA((SPAN,)),
            pltpu.SemaphoreType.DMA((SPAN,)),
            pltpu.SemaphoreType.DMA((SPAN,)),
            pltpu.SemaphoreType.DMA((SPAN + 1,)),
        ],
        compiler_params=pltpu.CompilerParams(
            collective_id=0, has_side_effects=True, vmem_limit_bytes=32 * 2**20
        ),
    )(normed.reshape(block_count, cluster, width), tables)
    arrived = arrived.reshape(SPAN * capacity, cluster, width)

    tile = pl.BlockSpec((group_rows, width), lambda i, s: (i, 0))
    weight = pl.BlockSpec((width, width), lambda i, s: (0, 0))
    return pl.pallas_call(
        attend_kernel,
        grid_spec=pltpu.PrefetchScalarGridSpec(
            num_scalar_prefetch=1,
            grid=(groups,),
            in_specs=[
                tile,
                tile,
                pl.BlockSpec(arrived.shape, lambda i, s: (0, 0, 0)),
            ]
            + [weight] * 5,
            out_specs=tile,
            scratch_shapes=[pltpu.VMEM((group_rows, width), bf16)] * 2,
        ),
        out_shape=jax.ShapeDtypeStruct((rows_dev, width), bf16),
        compiler_params=pltpu.CompilerParams(vmem_limit_bytes=48 * 2**20),
    )(slots, placed, normed, arrived, w_query, w_key, w_value, w_out, w_mix)


def solution(mesh):
    placed = (
        P(("groups", "elec"), None),
        P(("groups", "elec")),
        P(("groups", "elec"), None),
        P(),
        P(),
        P(),
        P(),
        P(),
    )
    return jax.shard_map(
        body, mesh=mesh, in_specs=placed, out_specs=P(("groups", "elec"), None), check_vma=False
    )
```

profile of v0, /device:TPU:12, one launch (start us, length us, event | category | flops | bytes accessed | tf_op | source)
XLA Modules:
  0.0 203.3 jit_solution(15862189000675266589)
XLA Ops:
  0.0 0.7 broadcast_subtract_fusion.1
  0.7 0.7 broadcast_subtract_fusion.local_ref
  1.4 0.8 copy.10
  2.2 0.1 reshape.197
  2.3 0.2 select_reduce_fusion.1
  2.5 0.2 select_reduce_fusion
  2.7 5.4 %shard_map.82 = (bf16[4096,256]{1,0:T(8,128)(2,1)}, bf16[4096,256]{1,0:T(8,128)(2,1)}) custom-call(s32[8,1,512]{2,1,0:T(1,128)} %broadcast_subtract_fusion.local_ref, bf16[4096,256]{1,0:T(8,128)(2,1)} %features_ref.1), custom_call_target="tpu_custom_call" | custom-call | tf_op jit(solution)/shard_map/pallas_call | solution.py:198
  8.1 0.0 copy-start.1
  8.1 1.6 copy-done.1
  9.7 0.0 copy-start.2
  9.7 0.0 copy-start.3
  9.7 0.0 copy-start.4
  9.7 0.0 copy-start.5
  9.7 0.0 copy-start.6
  9.7 0.0 copy-start.7
  9.7 0.0 copy-start.8
  9.7 149.1 %shard_map.83 = bf16[8,1600,256]{2,1,0:T(8,128)(2,1)S(1)} custom-call(bf16[64,64,256]{2,1,0:T(8,128)(2,1)S(1)} %bitcast.5, s32[8,1,128]{2,1,0:T(1,128)S(1)} %bitcast.6), custom_call_target="tpu_custom_call" | custom-call | tf_op jit(solution)/shard_map/pallas_call | solution.py:207
  158.9 0.0 copy-start
  158.9 2.7 %copy-done = bf16[8,1600,256]{2,1,0:T(8,128)(2,1)} copy-done((bf16[8,1600,256]{2,1,0:T(8,128)(2,1)}, bf16[8,1600,256]{2,1,0:T(8,128)(2,1)S(1)}, u32[]{:S(2)}) %copy-start) | copy-done | bytes 6553624
  161.6 0.0 copy-done.2
  161.6 0.0 copy-done.3
  161.6 0.0 copy-done.4
  161.6 0.0 copy-done.5
  161.6 0.0 copy-done.6
  161.6 0.0 copy-done.7
  161.7 0.0 copy-done.8
  161.7 41.7 %shard_map.84 = bf16[4096,256]{1,0:T(8,128)(2,1)} custom-call(s32[192]{0:T(256)S(1)} %get-tuple-element.10.slots_ref, bf16[4096,256]{1,0:T(8,128)(2,1)S(1)} %copy-done.3, bf16[4096,256]{1,0:T(8,128)(2,1)S(1)} %copy-done.2, bf16[200,64,256]{2,1,0:T(8,128)(2,1)} %bitcast.4, bf16[256,256]{1,0:T(8,128)(2,1)S(1)} %copy-done.4, bf16[256,256]{1,0:T(8,128)(2,1)S(1)} %copy-done.5, ...), custom_call_target="tpu_custom_call" | custom-call | tf_op jit(solution)/shard_map/pallas_call | solution.py:230
  (3 shorter events, 0.0 us)
Async XLA Ops:
  8.1 1.6 copy-start.1
  9.7 151.9 %copy-start.2 = (bf16[4096,256]{1,0:T(8,128)(2,1)S(1)}, bf16[4096,256]{1,0:T(8,128)(2,1)}, u32[]{:S(2)}) copy-start(bf16[4096,256]{1,0:T(8,128)(2,1)} %get-tuple-element.8.normed_ref) | copy-start | bytes 6291460
  9.7 151.9 %copy-start.3 = (bf16[4096,256]{1,0:T(8,128)(2,1)S(1)}, bf16[4096,256]{1,0:T(8,128)(2,1)}, u32[]{:S(2)}) copy-start(bf16[4096,256]{1,0:T(8,128)(2,1)} %get-tuple-element.7.placed_ref) | copy-start | bytes 6291460
  9.7 151.9 %copy-start.4 = (bf16[256,256]{1,0:T(8,128)(2,1)S(1)}, bf16[256,256]{1,0:T(8,128)(2,1)}, u32[]{:S(2)}) copy-start(bf16[256,256]{1,0:T(8,128)(2,1)} %wq_ref.1) | copy-start | bytes 393220
  9.7 151.9 %copy-start.5 = (bf16[256,256]{1,0:T(8,128)(2,1)S(1)}, bf16[256,256]{1,0:T(8,128)(2,1)}, u32[]{:S(2)}) copy-start(bf16[256,256]{1,0:T(8,128)(2,1)} %wk_ref.1) | copy-start | bytes 393220
  9.7 151.9 %copy-start.6 = (bf16[256,256]{1,0:T(8,128)(2,1)S(1)}, bf16[256,256]{1,0:T(8,128)(2,1)}, u32[]{:S(2)}) copy-start(bf16[256,256]{1,0:T(8,128)(2,1)} %wv_ref.1) | copy-start | bytes 393220
  9.7 151.9 %copy-start.7 = (bf16[256,256]{1,0:T(8,128)(2,1)S(1)}, bf16[256,256]{1,0:T(8,128)(2,1)}, u32[]{:S(2)}) copy-start(bf16[256,256]{1,0:T(8,128)(2,1)} %wo_ref.1) | copy-start | bytes 393220
  9.7 151.9 %copy-start.8 = (bf16[256,256]{1,0:T(8,128)(2,1)S(1)}, bf16[256,256]{1,0:T(8,128)(2,1)}, u32[]{:S(2)}) copy-start(bf16[256,256]{1,0:T(8,128)(2,1)} %wm_ref.1) | copy-start | bytes 393220
  158.9 2.7 %copy-start = (bf16[8,1600,256]{2,1,0:T(8,128)(2,1)}, bf16[8,1600,256]{2,1,0:T(8,128)(2,1)S(1)}, u32[]{:S(2)}) copy-start(bf16[8,1600,256]{2,1,0:T(8,128)(2,1)S(1)} %shard_map.83) | copy-start | bytes 19660804
where the time goes:
time: 204 us; the launch traced here: 203 us
  Pallas kernels  196 us (96%)
  local copies, waits for them, and re-layouts  5.26 us (3%)
    pallas_call x1, Pallas kernels, body(): pl.pallas_call(functools.partial(exchange_kernel, capacity, stride), in_s...  149 us
    pallas_call x1, Pallas kernels, body(): pl.pallas_call(attend_kernel, grid_spec=pltpu.PrefetchScalarGridSpec(num_...  41.7 us
    pallas_call x1, Pallas kernels, body(): pl.pallas_call(place_kernel, grid=(groups // batch,), in_specs=[pl.BlockS...  5.4 us
    unnamed x19, local copies, waits for them, and re-layouts  5.12 us

commit v1 on v0

--- a/solution.py
+++ b/solution.py
@@ -21,28 +21,131 @@
     return centred * lax.rsqrt(variance + 1e-05)
 
 
-def slot_table(listed, block_count, capacity, position, stride):
-    flattened = listed.reshape(-1)
-    owner_device = flattened // block_count
-    within = flattened % block_count
-    entries = flattened.shape[0]
-    offset = (position - owner_device // stride) % SPAN
-    alike = offset[:, None] == offset[None, :]
-    earlier = jnp.arange(entries)[None, :] < jnp.arange(entries)[:, None]
-    ranking = jnp.sum(jnp.where(alike & earlier, 1, 0), axis=1).astype(jnp.int32)
-    slots = offset * capacity + ranking
-    columns = jnp.arange(SPAN * LANES, dtype=jnp.int32)
-    matches = (offset * LANES + ranking)[None, :] == columns[:, None]
-    tables = jnp.sum(jnp.where(matches, within[None, :], 0), axis=1)
-    return slots, tables.astype(jnp.int32).reshape(SPAN, 1, LANES)
-
-
-def place_kernel(local_ref, features_ref, placed_ref, normed_ref):
-    groups, _, size = local_ref.shape
+def own_needs(listed, block_count, stride):
+    flat = listed.reshape(-1)
+    column = (flat // block_count // stride) * block_count + flat % block_count
+    columns = jnp.arange(SPAN * block_count, dtype=jnp.int32)
+    hit = column[None, :] == columns[:, None]
+    return column, jnp.max(jnp.where(hit, 1, 0), axis=1).astype(jnp.int32)
+
+
+def before(flags):
+    size = flags.shape[-1]
+    lower = (jnp.arange(size)[:, None] < jnp.arange(size)[None, :]).astype(jnp.bfloat16)
+    counts = jnp.dot(
+        flags.reshape(-1, size).astype(jnp.bfloat16), lower, preferred_element_type=jnp.float32
+    )
+    return counts.reshape(flags.shape).astype(jnp.int32)
+
+
+def invert(place, flags, values, size):
+    hit = (place[..., None, :] == jnp.arange(size, dtype=jnp.int32)[:, None]) & (
+        flags[..., None, :] > 0
+    )
+    return jnp.sum(jnp.where(hit, values[..., None, :], 0), axis=-1).astype(jnp.int32)
+
+
+def make_plan(needs, column, position, capacity):
+    blocks = needs.shape[-1]
+    owners = jnp.arange(SPAN, dtype=jnp.int32)
+    static = list(range(SPAN))
+    ends = [2 * (3 * (1 - o // 4)) + o % 2 for o in static]
+    first = jnp.stack([needs[ends[o] ^ 1, o] for o in static])
+    second = jnp.stack([needs[ends[o], o] for o in static]) * (1 - first)
+    third = 1 - first - second
+    c0, c1, c2 = before(first), before(second), before(third)
+    n0 = jnp.sum(first, axis=1, keepdims=True)
+    n1 = jnp.sum(second, axis=1, keepdims=True)
+    order = jnp.where(first > 0, c0, jnp.where(second > 0, n0 + c1, n0 + n1 + c2))
+    rank = before(needs)
+    within = jnp.arange(blocks, dtype=jnp.int32)
+
+    def at(array, index):
+        return lax.dynamic_index_in_dim(array, index, 0, keepdims=False)
+
+    near_readers = [position ^ t for t in range(4)]
+    mine = lax.dynamic_index_in_dim(needs, position, 1, keepdims=False)
+    mine_rank = lax.dynamic_index_in_dim(rank, position, 1, keepdims=False)
+    near = jnp.stack(
+        [
+            invert(at(mine_rank, q), at(mine, q), within, LANES)
+            for q in near_readers
+        ]
+    )
+    all_flags = jnp.ones((blocks,), jnp.int32)
+    far_list = invert(at(order, position), all_flags, within, LANES)
+
+    z, y = position // 2, position % 2
+    half = z // 2
+    inner = (z + half) % 2
+    partner_needs = at(needs, position ^ 1)
+    partner_rank = at(rank, position ^ 1)
+    sources = [2 * (2 - half) + y, 2 * (3 * (1 - half)) + y]
+    filters = jnp.stack(
+        [
+            invert(at(partner_rank, s), at(partner_needs, s), at(order, s), LANES)
+            for s in sources
+        ]
+    )
+    tables = jnp.concatenate([near, far_list[None], filters], axis=0)
+
+    my_rank = at(rank, position)
+    other = owners ^ position
+    oz = owners // 2
+    owner_inner = (oz + oz // 2) % 2
+    slot_index = 1 - owner_inner
+    far_base = (4 * capacity) + slot_index * blocks
+    side_base = (4 * capacity) + 2 * blocks + slot_index * capacity
+    near_loc = (other * capacity)[:, None] + my_rank
+    far_loc = far_base[:, None] + order
+    side_loc = side_base[:, None] + jnp.where(inner > 0, my_rank, order)
+    same_half = (owners // 4 == position // 4)[:, None]
+    same_line = (owners % 2 == y)[:, None]
+    location = jnp.where(same_half, near_loc, jnp.where(same_line, far_loc, side_loc)).reshape(-1)
+    hit = column[:, None] == jnp.arange(SPAN * blocks, dtype=jnp.int32)[None, :]
+    slots = jnp.sum(jnp.where(hit, location[None, :], 0), axis=1).astype(jnp.int32)
+    return slots, tables
+
+
+def place_kernel(
+    stride, assignment_ref, need_ref, features_ref, placed_ref, normed_ref, needs_ref,
+    landing, s_send, s_recv,
+):
+    groups, _, size = assignment_ref.shape
+    me = lax.axis_index("elec")
+    group = lax.axis_index("groups")
+    peers = lax.axis_size("elec")
+    position = me // stride
+    step_index = pl.program_id(0)
+
+    def toward(step):
+        return (group, lax.rem(me + step * stride, peers))
+
+    def ask(step):
+        return pltpu.make_async_remote_copy(
+            src_ref=need_ref, dst_ref=landing.at[step],
+            send_sem=s_send.at[step], recv_sem=s_recv.at[step],
+            device_id=toward(step), device_id_type=MESH,
+        )
+
+    @pl.when(step_index == 0)
+    def _():
+        barrier = pltpu.get_barrier_semaphore()
+        for step in range(1, SPAN):
+            pl.semaphore_signal(barrier, inc=1, device_id=toward(step), device_id_type=MESH)
+        pl.semaphore_wait(barrier, SPAN - 1)
+        for step in range(1, SPAN):
+            ask(step).start()
+        landing[0] = need_ref[...]
+
     lane = lax.broadcasted_iota(jnp.int32, (size, LANES), 1).astype(jnp.float32)
     for i in range(groups):
         rows = pl.ds(i * size, size)
-        takes = jnp.broadcast_to(local_ref[i].astype(jnp.float32), (LANES, size)).T
+        base = me * (features_ref.shape[0] * pl.num_programs(0)) + (
+            (step_index * groups + i) * size
+        )
+        local = (assignment_ref[i] - base).astype(jnp.float32)
+        takes = jnp.broadcast_to(local, (LANES, size)).T
         one_hot = jnp.concatenate(
             [jnp.where(takes == lane + k, 1.0, 0.0) for k in range(0, size, LANES)], axis=1
         ).astype(jnp.bfloat16)
@@ -50,65 +153,157 @@
         placed_ref[rows, :] = placed.astype(jnp.bfloat16)
         normed_ref[rows, :] = layer_norm(placed).astype(jnp.bfloat16)
 
+    @pl.when(step_index == pl.num_programs(0) - 1)
+    def _():
+        for step in range(1, SPAN):
+            ask(step).wait()
+        for q in range(SPAN):
+            needs_ref[q] = landing[lax.rem(position - q + SPAN, SPAN)]
+
 
 def exchange_kernel(
-    capacity, stride, blocks_ref, tables_ref, arrived_ref,
-    wanted, wanted_s, outbox, t_send, t_recv, d_send, d_recv, local_sem,
+    capacity, stride, tables_ref, blocks_ref, arrived_ref,
+    out_near, out_far, out_side, far0, far1,
+    n_send, n_recv, l_send, f_send, f_recv, w_send, p_send, p_recv, local_sem,
 ):
     me = lax.axis_index("elec")
     group = lax.axis_index("groups")
+    position = me // stride
+    rest = lax.rem(me, stride)
+    block_count = blocks_ref.shape[0]
+    cap = capacity
+    z, y = position // 2, lax.rem(position, 2)
+    half = z // 2
+    inner = lax.rem(z + half, 2)
+    pair_z = z + 1 - 2 * lax.rem(z, 2)
+    pair_y = 1 - y
+
+    def device(zz, yy):
+        return (group, (2 * zz + yy) * stride + rest)
+
+    near_devices = [device(z, pair_y), device(pair_z, y), device(pair_z, pair_y)]
+    far_inner = device(2 - half, y)
+
+    barrier = pltpu.get_barrier_semaphore()
     peers = lax.axis_size("elec")
-    cluster = blocks_ref.shape[1]
-
-    def toward(step):
-        return (group, lax.rem(me + step * stride + peers, peers))
-
-    barrier = pltpu.get_barrier_semaphore()
     for step in range(1, SPAN):
-        pl.semaphore_signal(barrier, inc=1, device_id=toward(step), device_id_type=MESH)
+        pl.semaphore_signal(
+            barrier, inc=1, device_id=(group, lax.rem(me + step * stride, peers)),
+            device_id_type=MESH,
+        )
     pl.semaphore_wait(barrier, SPAN - 1)
 
-    order = sorted(range(1, SPAN), key=lambda s: abs(s - SPAN // 2))
-    asks = {}
-    for step in order:
-        asks[step] = pltpu.make_async_remote_copy(
-            src_ref=tables_ref.at[step], dst_ref=wanted.at[step],
-            send_sem=t_send.at[step], recv_sem=t_recv.at[step],
-            device_id=toward(-step), device_id_type=MESH,
-        )
-        asks[step].start()
-
-    def gather(step, source):
-        copy = pltpu.make_async_copy(source, wanted_s.at[step], local_sem.at[step])
-        copy.start()
-        copy.wait()
-
+    far = [far0, far1]
+    chunks = [(0, cap), (cap, cap), (2 * cap, block_count - 2 * cap)]
+
+    def gather(row, first, count, source, target, base):
         def one(k, carry):
-            start = pl.multiple_of(k * cluster, cluster)
-            outbox[step, pl.ds(start, cluster), :] = blocks_ref[wanted_s[step, 0, k]]
+            target[base + first + k] = source[tables_ref[row, first + k]]
             return carry
 
-        lax.fori_loop(0, capacity, one, 0)
-
-    sends = []
-    for step in order:
-        asks[step].wait_recv()
-        gather(step, wanted.at[step])
-        send = pltpu.make_async_remote_copy(
-            src_ref=outbox.at[step], dst_ref=arrived_ref.at[step],
-            send_sem=d_send.at[step], recv_sem=d_recv.at[step],
-            device_id=toward(step), device_id_type=MESH,
-        )
-        send.start()
-        sends.append(send)
-    gather(0, tables_ref.at[0])
-    own = pltpu.make_async_copy(outbox.at[0], arrived_ref.at[0], local_sem.at[SPAN])
+        lax.fori_loop(0, count, one, 0)
+
+    def far_copy(s, c):
+        start, count = chunks[c]
+        return pltpu.make_async_remote_copy(
+            src_ref=out_far.at[pl.ds(start, count)], dst_ref=far[s].at[pl.ds(start, count)],
+            send_sem=l_send.at[c], recv_sem=f_recv.at[s, c],
+            device_id=far_inner, device_id_type=MESH,
+        )
+
+    def forward_copy(s, c):
+        start, count = chunks[c]
+        return pltpu.make_async_remote_copy(
+            src_ref=far[s].at[pl.ds(start, count)], dst_ref=far[s].at[pl.ds(start, count)],
+            send_sem=f_send.at[s, c], recv_sem=f_recv.at[s, c],
+            device_id=near_devices[1], device_id_type=MESH,
+        )
+
+    side_base = 4 * cap + 2 * block_count
+
+    def side_copy(s, source):
+        return pltpu.make_async_remote_copy(
+            src_ref=source, dst_ref=arrived_ref.at[pl.ds(side_base + s * cap, cap)],
+            send_sem=p_send.at[s], recv_sem=p_recv.at[s],
+            device_id=near_devices[0], device_id_type=MESH,
+        )
+
+    def near_copy(t):
+        return pltpu.make_async_remote_copy(
+            src_ref=out_near.at[pl.ds(t * cap, cap)], dst_ref=arrived_ref.at[pl.ds(t * cap, cap)],
+            send_sem=n_send.at[t], recv_sem=n_recv.at[t],
+            device_id=near_devices[t - 1], device_id_type=MESH,
+        )
+
+    def send_far(c):
+        gather(4, chunks[c][0], chunks[c][1], blocks_ref, out_far, 0)
+
+        @pl.when(inner == 1)
+        def _():
+            far_copy(0, c).start()
+
+        @pl.when(inner == 0)
+        def _():
+            far_copy(1, c).start()
+
+    def send_near(t):
+        gather(t, 0, cap, blocks_ref, out_near, t * cap)
+        near_copy(t).start()
+
+    send_far(0)
+    send_near(2)
+    send_near(3)
+    send_far(1)
+    send_far(2)
+    send_near(1)
+    gather(0, 0, cap, blocks_ref, out_near, 0)
+    own = pltpu.make_async_copy(
+        out_near.at[pl.ds(0, cap)], arrived_ref.at[pl.ds(0, cap)], local_sem.at[0]
+    )
     own.start()
-    for step in order:
-        asks[step].wait_send()
+
+    def keep(s, count):
+        return pltpu.make_async_copy(
+            far[s].at[pl.ds(0, count)],
+            arrived_ref.at[pl.ds(4 * cap + s * block_count, count)], local_sem.at[1 + s],
+        )
+
+    @pl.when(inner == 1)
+    def _():
+        for c in range(2):
+            for s in range(2):
+                far_copy(s, c).wait_recv()
+                forward_copy(s, c).start()
+        for s in range(2):
+            far_copy(s, 2).wait_recv()
+            gather(5 + s, 0, cap, far[s], out_side, s * cap)
+            side_copy(s, out_side.at[pl.ds(s * cap, cap)]).start()
+            keep(s, block_count).start()
+        for s in range(2):
+            for c in range(2):
+                forward_copy(s, c).wait_send()
+            keep(s, block_count).wait()
+            side_copy(s, out_side.at[pl.ds(s * cap, cap)]).wait_send()
+
+    @pl.when(inner == 0)
+    def _():
+        for s in range(2):
+            far_copy(s, 0).wait_recv()
+            side_copy(s, far[s].at[pl.ds(0, cap)]).start()
+        for s in range(2):
+            far_copy(s, 1).wait_recv()
+            keep(s, 2 * cap).start()
+        for s in range(2):
+            keep(s, 2 * cap).wait()
+            side_copy(s, far[s].at[pl.ds(0, cap)]).wait_send()
+
     own.wait()
-    for send in sends:
-        send.wait()
+    for c in range(3):
+        far_copy(0, c).wait_send()
+    for t in range(1, 4):
+        near_copy(t).wait()
+    for s in range(2):
+        side_copy(s, out_side.at[pl.ds(s * cap, cap)]).wait_recv()
 
 
 def attend_kernel(
@@ -185,45 +380,69 @@
     cluster = rows_dev // block_count
     capacity = (block_count * pair_count + SPAN - 1) // SPAN + 1
     stride = lax.axis_size("elec") // SPAN
-    device_index = lax.axis_index("elec")
-    position = device_index // stride
+    position = lax.axis_index("elec") // stride
     group_rows = SPAN * cluster
     groups = rows_dev // group_rows
     bf16 = jnp.bfloat16
 
-    local = (assignment - device_index * rows_dev).reshape(groups, 1, group_rows)
-    local = local - group_rows * jnp.arange(groups, dtype=jnp.int32)[:, None, None]
+    column, need = own_needs(pairs, block_count, stride)
+    need_rows = SPAN * block_count // LANES
     batch = math.gcd(groups, 2)
     tile = pl.BlockSpec((batch * group_rows, width), lambda i: (i, 0))
-    placed, normed = pl.pallas_call(
-        place_kernel,
+    placed, normed, needs = pl.pallas_call(
+        functools.partial(place_kernel, stride),
         grid=(groups // batch,),
-        in_specs=[pl.BlockSpec((batch, 1, group_rows), lambda i: (i, 0, 0)), tile],
-        out_specs=[tile, tile],
-        out_shape=[jax.ShapeDtypeStruct((rows_dev, width), bf16)] * 2,
-    )(local, features)
-
-    slots, tables = slot_table(pairs, block_count, capacity, position, stride)
+        in_specs=[
+            pl.BlockSpec((batch, 1, group_rows), lambda i: (i, 0, 0)),
+            pl.BlockSpec((need_rows, LANES), lambda i: (0, 0)),
+            tile,
+        ],
+        out_specs=[tile, tile, pl.BlockSpec((SPAN, need_rows, LANES), lambda i: (0, 0, 0))],
+        out_shape=[jax.ShapeDtypeStruct((rows_dev, width), bf16)] * 2
+        + [jax.ShapeDtypeStruct((SPAN, need_rows, LANES), jnp.int32)],
+        scratch_shapes=[
+            pltpu.VMEM((SPAN, need_rows, LANES), jnp.int32),
+            pltpu.SemaphoreType.DMA((SPAN,)),
+            pltpu.SemaphoreType.DMA((SPAN,)),
+        ],
+        compiler_params=pltpu.CompilerParams(collective_id=1, has_side_effects=True),
+    )(
+        assignment.reshape(groups, 1, group_rows), need.reshape(need_rows, LANES), features
+    )
+
+    slots, tables = make_plan(
+        needs.reshape(SPAN, SPAN, block_count), column, position, capacity
+    )
+    total = 6 * capacity + 2 * block_count
+    block = (cluster, width)
     arrived = pl.pallas_call(
         functools.partial(exchange_kernel, capacity, stride),
-        in_specs=[pl.BlockSpec(memory_space=pltpu.VMEM)] * 2,
+        in_specs=[
+            pl.BlockSpec(memory_space=pltpu.SMEM),
+            pl.BlockSpec(memory_space=pltpu.VMEM),
+        ],
         out_specs=pl.BlockSpec(memory_space=pl.ANY),
-        out_shape=jax.ShapeDtypeStruct((SPAN, capacity * cluster, width), bf16),
+        out_shape=jax.ShapeDtypeStruct((total,) + block, bf16),
         scratch_shapes=[
-            pltpu.VMEM((SPAN, 1, LANES), jnp.int32),
-            pltpu.SMEM((SPAN, 1, LANES), jnp.int32),
-            pltpu.VMEM((SPAN, capacity * cluster, width), bf16),
-            pltpu.SemaphoreType.DMA((SPAN,)),
-            pltpu.SemaphoreType.DMA((SPAN,)),
-            pltpu.SemaphoreType.DMA((SPAN,)),
-            pltpu.SemaphoreType.DMA((SPAN,)),
-            pltpu.SemaphoreType.DMA((SPAN + 1,)),
+            pltpu.VMEM((4 * capacity,) + block, bf16),
+            pltpu.VMEM((block_count,) + block, bf16),
+            pltpu.VMEM((2 * capacity,) + block, bf16),
+            pltpu.VMEM((block_count,) + block, bf16),
+            pltpu.VMEM((block_count,) + block, bf16),
+            pltpu.SemaphoreType.DMA((4,)),
+            pltpu.SemaphoreType.DMA((4,)),
+            pltpu.SemaphoreType.DMA((3,)),
+            pltpu.SemaphoreType.DMA((2, 3)),
+            pltpu.SemaphoreType.DMA((2, 3)),
+            pltpu.SemaphoreType.DMA((2,)),
+            pltpu.SemaphoreType.DMA((2,)),
+            pltpu.SemaphoreType.DMA((2,)),
+            pltpu.SemaphoreType.DMA((3,)),
         ],
         compiler_params=pltpu.CompilerParams(
             collective_id=0, has_side_effects=True, vmem_limit_bytes=32 * 2**20
         ),
-    )(normed.reshape(block_count, cluster, width), tables)
-    arrived = arrived.reshape(SPAN * capacity, cluster, width)
+    )(tables, normed.reshape(block_count, cluster, width))
 
     tile = pl.BlockSpec((group_rows, width), lambda i, s: (i, 0))
     weight = pl.BlockSpec((width, width), lambda i, s: (0, 0))

time: 204 us -> 192 us (0.941)
  Pallas kernels: 196 us -> 182 us
    pallas_call x1, Pallas kernels: 149 us -> 131 us  [body(): pl.pallas_call(functools.partial(exchange_kernel, capacity, stride), in_s...]
    pallas_call x1, Pallas kernels: 5.4 us -> 8.76 us  [body(): pl.pallas_call(functools.partial(place_kernel, stride), grid=(groups // b...]
where the time goes in v1:
time: 192 us; the launch traced here: 191 us
  Pallas kernels  182 us (95%)
  local copies, waits for them, and re-layouts  7.02 us (4%)
    pallas_call x1, Pallas kernels, body(): pl.pallas_call(functools.partial(exchange_kernel, capacity, stride), in_s...  131 us
    pallas_call x1, Pallas kernels, body(): pl.pallas_call(attend_kernel, grid_spec=pltpu.PrefetchScalarGridSpec(num_...  42.4 us
    pallas_call x1, Pallas kernels, body(): pl.pallas_call(functools.partial(place_kernel, stride), grid=(groups // b...  8.76 us
    unnamed x19, local copies, waits for them, and re-layouts  5.89 us

profile of v1, /device:TPU:12, one launch (start us, length us, event | category | flops | bytes accessed | tf_op | source)
XLA Modules:
  0.0 191.0 jit_solution(14049463479700233853)
XLA Ops:
  0.0 0.8 copy.10
  0.8 0.1 reshape.301
  1.0 0.7 select_reduce_fusion.1
  1.7 8.8 %shard_map.82 = (bf16[4096,256]{1,0:T(8,128)(2,1)}, bf16[4096,256]{1,0:T(8,128)(2,1)}, s32[8,4,128]{2,1,0:T(4,128)}) custom-call(s32[8,1,512]{2,1,0:T(1,128)} %bitcast.87, s32[4,128]{1,0:T(4,128)} %bitcast.88, bf16[4096,256]{1,0:T(8,128)(2,1)} %features_ref.1), custom_call_target="tpu_custom_call" | custom-call | tf_op jit(solution)/shard_map/pallas_call | solution.py:392
  10.5 0.8 reshape_reshape.3
  11.3 0.1 convolution_convert_fusion
  11.5 0.1 select_reduce_fusion.5
  11.6 0.1 select_reduce_fusion.7
  11.7 0.1 fusion.19
  11.9 0.1 fusion
  12.0 0.1 fusion.3
  12.1 0.1 fusion.13
  12.2 0.1 broadcast_in_dim.140
  12.3 0.3 select_reduce_fusion.slots_ref
  12.6 0.1 select_reduce_fusion.3
  12.7 0.1 select_reduce_fusion.2
  12.8 0.1 select_reduce_fusion.4
  12.9 0.0 copy-start.1
  12.9 1.6 copy-done.1
  14.5 0.0 copy-start.2
  14.5 0.0 copy-start.3
  14.5 0.0 copy-start.4
  14.5 0.0 copy-start.5
  14.5 0.0 copy-start.6
  14.6 0.0 copy-start.7
  14.6 0.0 copy-start.8
  14.6 130.5 %shard_map.83.arrived_ref = bf16[278,64,256]{2,1,0:T(8,128)(2,1)S(1)} custom-call(s32[7,128]{1,0:T(8,128)S(1)} %concatenate.3.tables_ref, bf16[64,64,256]{2,1,0:T(8,128)(2,1)S(1)} %bitcast.86), custom_call_target="tpu_custom_call" | custom-call | tf_op jit(solution)/shard_map/pallas_call | solution.py:418
  145.1 0.0 copy-start
  145.1 3.5 %copy-done = bf16[278,64,256]{2,1,0:T(8,128)(2,1)} copy-done((bf16[278,64,256]{2,1,0:T(8,128)(2,1)}, bf16[278,64,256]{2,1,0:T(8,128)(2,1)S(1)}, u32[]{:S(2)}) %copy-start) | copy-done | bytes 9109528
  148.6 0.0 copy-done.2
  148.6 0.0 copy-done.3
  148.6 0.0 copy-done.4
  148.6 0.0 copy-done.5
  148.6 0.0 copy-done.6
  148.6 0.0 copy-done.7
  148.6 0.0 copy-done.8
  148.6 42.4 %shard_map.84 = bf16[4096,256]{1,0:T(8,128)(2,1)} custom-call(s32[192]{0:T(256)S(1)} %select_reduce_fusion.slots_ref, bf16[4096,256]{1,0:T(8,128)(2,1)S(1)} %copy-done.3, bf16[4096,256]{1,0:T(8,128)(2,1)S(1)} %copy-done.2, bf16[278,64,256]{2,1,0:T(8,128)(2,1)} %copy-done, bf16[256,256]{1,0:T(8,128)(2,1)S(1)} %copy-done.4, bf16[256,256]{1,0:T(8,128)(2,1)S(1)} %copy-done.5, ...), custom_call_target="tpu_custom_call" | custom-call | tf_op jit(solution)/shard_map/pallas_call | solution.py:449
  (12 shorter events, 0.2 us)
Async XLA Ops:
  12.9 1.6 copy-start.1
  14.5 134.1 %copy-start.2 = (bf16[4096,256]{1,0:T(8,128)(2,1)S(1)}, bf16[4096,256]{1,0:T(8,128)(2,1)}, u32[]{:S(2)}) copy-start(bf16[4096,256]{1,0:T(8,128)(2,1)} %get-tuple-element.10.normed_ref) | copy-start | bytes 6291460
  14.5 134.1 %copy-start.3 = (bf16[4096,256]{1,0:T(8,128)(2,1)S(1)}, bf16[4096,256]{1,0:T(8,128)(2,1)}, u32[]{:S(2)}) copy-start(bf16[4096,256]{1,0:T(8,128)(2,1)} %get-tuple-element.9.placed_ref) | copy-start | bytes 6291460
  14.5 134.1 %copy-start.4 = (bf16[256,256]{1,0:T(8,128)(2,1)S(1)}, bf16[256,256]{1,0:T(8,128)(2,1)}, u32[]{:S(2)}) copy-start(bf16[256,256]{1,0:T(8,128)(2,1)} %wq_ref.1) | copy-start | bytes 393220
  14.5 134.1 %copy-start.5 = (bf16[256,256]{1,0:T(8,128)(2,1)S(1)}, bf16[256,256]{1,0:T(8,128)(2,1)}, u32[]{:S(2)}) copy-start(bf16[256,256]{1,0:T(8,128)(2,1)} %wk_ref.1) | copy-start | bytes 393220
  14.5 134.1 %copy-start.6 = (bf16[256,256]{1,0:T(8,128)(2,1)S(1)}, bf16[256,256]{1,0:T(8,128)(2,1)}, u32[]{:S(2)}) copy-start(bf16[256,256]{1,0:T(8,128)(2,1)} %wv_ref.1) | copy-start | bytes 393220
  14.6 134.1 %copy-start.7 = (bf16[256,256]{1,0:T(8,128)(2,1)S(1)}, bf16[256,256]{1,0:T(8,128)(2,1)}, u32[]{:S(2)}) copy-start(bf16[256,256]{1,0:T(8,128)(2,1)} %wo_ref.1) | copy-start | bytes 393220
  14.6 134.1 %copy-start.8 = (bf16[256,256]{1,0:T(8,128)(2,1)S(1)}, bf16[256,256]{1,0:T(8,128)(2,1)}, u32[]{:S(2)}) copy-start(bf16[256,256]{1,0:T(8,128)(2,1)} %wm_ref.1) | copy-start | bytes 393220
  145.1 3.5 %copy-start = (bf16[278,64,256]{2,1,0:T(8,128)(2,1)}, bf16[278,64,256]{2,1,0:T(8,128)(2,1)S(1)}, u32[]{:S(2)}) copy-start(bf16[278,64,256]{2,1,0:T(8,128)(2,1)S(1)} %shard_map.83.arrived_ref) | copy-start | bytes 27328516

commit v2 on v1

v2 whole, which is shorter than its diff:
```python
import functools
import math

import jax
import jax.numpy as jnp
from jax import lax
from jax.experimental import pallas as pl
from jax.experimental.pallas import tpu as pltpu
from jax.sharding import PartitionSpec as P

HEADS = 16
SPAN = 8
LANES = 128
MESH = pl.DeviceIdType.MESH


def layer_norm(rows):
    mean = jnp.mean(rows, axis=-1, keepdims=True)
    centred = rows - mean
    variance = jnp.mean(centred * centred, axis=-1, keepdims=True)
    return centred * lax.rsqrt(variance + 1e-05)


def own_needs(listed, block_count, stride):
    flat = listed.reshape(-1)
    column = (flat // block_count // stride) * block_count + flat % block_count
    columns = jnp.arange(SPAN * block_count, dtype=jnp.int32)
    hit = column[None, :] == columns[:, None]
    return column, jnp.max(jnp.where(hit, 1, 0), axis=1).astype(jnp.int32)


def before(flags):
    size = flags.shape[-1]
    lower = (jnp.arange(size)[:, None] < jnp.arange(size)[None, :]).astype(jnp.bfloat16)
    counts = jnp.dot(
        flags.reshape(-1, size).astype(jnp.bfloat16), lower, preferred_element_type=jnp.float32
    )
    return counts.reshape(flags.shape).astype(jnp.int32)


def invert(place, flags, values, size):
    hit = (place[..., None, :] == jnp.arange(size, dtype=jnp.int32)[:, None]) & (
        flags[..., None, :] > 0
    )
    return jnp.sum(jnp.where(hit, values[..., None, :], 0), axis=-1).astype(jnp.int32)


def make_plan(needs, column, position, capacity, pair_count):
    blocks = needs.shape[-1]
    owners = jnp.arange(SPAN, dtype=jnp.int32)
    static = list(range(SPAN))
    ends = [2 * (3 * (1 - o // 4)) + o % 2 for o in static]
    first = jnp.stack([needs[ends[o] ^ 1, o] for o in static])
    second = jnp.stack([needs[ends[o], o] for o in static]) * (1 - first)
    third = 1 - first - second
    c0, c1, c2 = before(first), before(second), before(third)
    n0 = jnp.sum(first, axis=1, keepdims=True)
    n1 = jnp.sum(second, axis=1, keepdims=True)
    order = jnp.where(first > 0, c0, jnp.where(second > 0, n0 + c1, n0 + n1 + c2))
    rank = before(needs)
    within = jnp.arange(blocks, dtype=jnp.int32)

    def at(array, index):
        return lax.dynamic_index_in_dim(array, index, 0, keepdims=False)

    mine = lax.dynamic_index_in_dim(needs, position, 1, keepdims=False)
    mine_rank = lax.dynamic_index_in_dim(rank, position, 1, keepdims=False)
    near = jnp.stack(
        [
            invert(at(mine_rank, position ^ t), at(mine, position ^ t), within, LANES)
            for t in range(1, 4)
        ]
    )
    all_flags = jnp.ones((blocks,), jnp.int32)
    far_list = invert(at(order, position), all_flags, within, LANES)

    z, y = position // 2, position % 2
    half = z // 2
    inner = (z + half) % 2
    partner_needs = at(needs, position ^ 1)
    partner_rank = at(rank, position ^ 1)
    sources = [2 * (2 - half) + y, 2 * (3 * (1 - half)) + y]
    filters = jnp.stack(
        [
            invert(at(partner_rank, s), at(partner_needs, s), at(order, s), LANES)
            for s in sources
        ]
    )
    tables = jnp.concatenate([near, far_list[None], filters], axis=0)

    my_rank = at(rank, position)
    oz = owners // 2
    outer_owner = 1 - (oz + oz // 2) % 2
    same_half = owners // 4 == position // 4
    same_line = owners % 2 == y
    source_group = jnp.where(
        same_half, owners ^ position, jnp.where(same_line, 4 + outer_owner, 6 + outer_owner)
    )
    location = jnp.where(
        (owners == position)[:, None],
        within[None, :],
        jnp.where(
            same_half[:, None] | ((inner > 0) & ~same_line)[:, None], my_rank, order
        ),
    )
    hit = column[:, None] == jnp.arange(SPAN * blocks, dtype=jnp.int32)[None, :]
    groups = jnp.broadcast_to(source_group[:, None], location.shape)
    packed = (groups * blocks + location).reshape(-1)
    packed = jnp.sum(jnp.where(hit, packed[None, :], 0), axis=1)
    entries = column.shape[0]
    group, key = packed // blocks, packed % blocks
    steps = jnp.arange(entries, dtype=jnp.int32)
    earlier = (group[:, None] == group[None, :]) & (steps[None, :] < steps[:, None])
    slots = group * capacity + jnp.sum(jnp.where(earlier, 1, 0), axis=1)
    slot_hit = slots[None, :] == jnp.arange(SPAN * capacity, dtype=jnp.int32)[:, None]
    jobs = jnp.sum(
        jnp.where(slot_hit, ((steps // pair_count) * blocks + key)[None, :], 0), axis=1
    )
    return (
        tables,
        (jobs // blocks).astype(jnp.int32),
        (jobs % blocks).astype(jnp.int32),
        (slots + blocks).astype(jnp.int32),
    )


def head_step(width):
    return -(-(width // HEADS + 2) // 8) * 8


def place_kernel(
    stride, assignment_ref, need_ref, features_ref, placed_ref, normed_ref, needs_ref,
    landing, s_send, s_recv,
):
    groups, _, size = assignment_ref.shape
    me = lax.axis_index("elec")
    group = lax.axis_index("groups")
    peers = lax.axis_size("elec")
    position = me // stride
    step_index = pl.program_id(0)

    def toward(step):
        return (group, lax.rem(me + step * stride, peers))

    def ask(step):
        return pltpu.make_async_remote_copy(
            src_ref=need_ref, dst_ref=landing.at[step],
            send_sem=s_send.at[step], recv_sem=s_recv.at[step],
            device_id=toward(step), device_id_type=MESH,
        )

    @pl.when(step_index == 0)
    def _():
        barrier = pltpu.get_barrier_semaphore()
        for step in range(1, SPAN):
            pl.semaphore_signal(barrier, inc=1, device_id=toward(step), device_id_type=MESH)
        pl.semaphore_wait(barrier, SPAN - 1)
        for step in range(1, SPAN):
            ask(step).start()
        landing[0] = need_ref[...]

    lane = lax.broadcasted_iota(jnp.int32, (size, LANES), 1).astype(jnp.float32)
    for i in range(groups):
        rows = pl.ds(i * size, size)
        base = me * (features_ref.shape[0] * pl.num_programs(0)) + (
            (step_index * groups + i) * size
        )
        local = (assignment_ref[i] - base).astype(jnp.float32)
        takes = jnp.broadcast_to(local, (LANES, size)).T
        one_hot = jnp.concatenate(
            [jnp.where(takes == lane + k, 1.0, 0.0) for k in range(0, size, LANES)], axis=1
        ).astype(jnp.bfloat16)
        placed = jnp.dot(one_hot, features_ref[rows, :], preferred_element_type=jnp.float32)
        placed_ref[rows, :] = placed.astype(jnp.bfloat16)
        normed_ref[rows, :] = layer_norm(placed).astype(jnp.bfloat16)

    @pl.when(step_index == pl.num_programs(0) - 1)
    def _():
        for step in range(1, SPAN):
            ask(step).wait()
        for q in range(SPAN):
            needs_ref[q] = landing[lax.rem(position - q + SPAN, SPAN)]


def layer_kernel(
    capacity, stride, pair_count,
    tables_ref, reader_ref, key_ref, slot_ref,
    blocks_ref, placed_ref, wq_ref, wk_ref, wv_ref, wo_ref, wm_ref,
    out_ref,
    near1, near2, near3, far0, far1, side0, side1, out_near, out_far, out_side,
    queries, wv_turned, wo_sorted, parts, attended,
    n_send, n_recv, l_send, f_send, f_recv, p_send, p_recv,
):
    f32, bf16 = jnp.float32, jnp.bfloat16
    me = lax.axis_index("elec")
    group = lax.axis_index("groups")
    peers = lax.axis_size("elec")
    position = me // stride
    rest = lax.rem(me, stride)
    block_count, cluster, width = blocks_ref.shape
    head_width = width // HEADS
    cap = capacity
    z, y = position // 2, lax.rem(position, 2)
    half = z // 2
    inner = lax.rem(z + half, 2)
    pair_z = z + 1 - 2 * lax.rem(z, 2)
    pair_y = 1 - y

    def device(zz, yy):
        return (group, (2 * zz + yy) * stride + rest)

    near_devices = [device(z, pair_y), device(pair_z, y), device(pair_z, pair_y)]
    far_inner = device(2 - half, y)
    near, far, side = [near1, near2, near3], [far0, far1], [side0, side1]
    chunks = [(0, cap), (cap, cap), (2 * cap, block_count - 2 * cap)]

    barrier = pltpu.get_barrier_semaphore()
    for step in range(1, SPAN):
        pl.semaphore_signal(
            barrier, inc=1, device_id=(group, lax.rem(me + step * stride, peers)),
            device_id_type=MESH,
        )
    pl.semaphore_wait(barrier, SPAN - 1)

    def gather(row, first, count, source, target, base):
        def one(k, carry):
            target[base + first + k] = source[tables_ref[row, first + k]]
            return carry

        lax.fori_loop(0, count, one, 0)

    def far_copy(s, c):
        start, count = chunks[c]
        return pltpu.make_async_remote_copy(
            src_ref=out_far.at[pl.ds(start, count)], dst_ref=far[s].at[pl.ds(start, count)],
            send_sem=l_send.at[c], recv_sem=f_recv.at[s, c],
            device_id=far_inner, device_id_type=MESH,
        )

    def forward_copy(s, c):
        start, count = chunks[c]
        return pltpu.make_async_remote_copy(
            src_ref=far[s].at[pl.ds(start, count)], dst_ref=far[s].at[pl.ds(start, count)],
            send_sem=f_send.at[s, c], recv_sem=f_recv.at[s, c],
            device_id=near_devices[1], device_id_type=MESH,
        )

    def side_copy(s, source):
        return pltpu.make_async_remote_copy(
            src_ref=source, dst_ref=side[s], send_sem=p_send.at[s], recv_sem=p_recv.at[s],
            device_id=near_devices[0], device_id_type=MESH,
        )

    def filtered(s):
        return side_copy(s, out_side.at[pl.ds(s * cap, cap)])

    def passed_on(s):
        return side_copy(s, far[s].at[pl.ds(0, cap)])

    def near_copy(t):
        return pltpu.make_async_remote_copy(
            src_ref=out_near.at[pl.ds((t - 1) * cap, cap)], dst_ref=near[t - 1],
            send_sem=n_send.at[t - 1], recv_sem=n_recv.at[t - 1],
            device_id=near_devices[t - 1], device_id_type=MESH,
        )

    def send_near(t):
        gather(t - 1, 0, cap, blocks_ref, out_near, (t - 1) * cap)
        near_copy(t).start()

    def send_far(s, c):
        gather(3, chunks[c][0], chunks[c][1], blocks_ref, out_far, 0)
        far_copy(s, c).start()

    @pl.when(inner == 1)
    def _():
        for c in range(3):
            send_far(0, c)

    for t in (2, 3, 1):
        send_near(t)

    lane = lax.broadcasted_iota(jnp.int32, (cluster, LANES), 1)
    per = LANES // 2 // head_width
    chosen = [
        jnp.where(lane // head_width == c, 1.0, 0.0).astype(bf16) for c in range(2 * per)
    ]
    low = lax.broadcasted_iota(jnp.int32, (head_width, LANES), 1) < cluster
    scale = math.log2(math.e) / head_width**0.5
    turned = (((1,), (1,)), ((), ()))

    def unit(size):
        row = lax.broadcasted_iota(jnp.int32, (size, size), 0)
        column = lax.broadcasted_iota(jnp.int32, (size, size), 1)
        return jnp.where(row == column, 1.0, 0.0).astype(bf16)

    wv_turned[...] = lax.dot_general(
        unit(width), wv_ref[...], turned, preferred_element_type=f32
    ).astype(bf16)
    for h in range(HEADS):
        start = (h % 2) * (width // 2) + (h // 2) * head_width
        wo_sorted[start : start + head_width, :] = wo_ref[
            h * head_width : (h + 1) * head_width, :
        ]

    def project(i, carry):
        rows = blocks_ref[pl.ds(i * SPAN, SPAN)].reshape(SPAN * cluster, width)
        result = jnp.dot(rows, wq_ref[...], preferred_element_type=f32) * scale
        queries[pl.ds(i * SPAN, SPAN)] = result.astype(bf16).reshape(SPAN, cluster, width)
        return carry

    lax.fori_loop(0, block_count // SPAN, project, 0)

    def several(places, query_blocks, key_blocks):
        count = len(places)
        keys = jnp.dot(
            jnp.concatenate(key_blocks, axis=0), wk_ref[...], preferred_element_type=f32
        ).astype(bf16)
        values = [
            lax.dot_general(wv_turned[...], rows, turned, preferred_element_type=f32).astype(bf16)
            for rows in key_blocks
        ]
        scores = []
        for i in range(count):
            for g in range(HEADS // per):
                band = (g // 2) * LANES
                query = query_blocks[i][:, band : band + LANES]
                stacked = jnp.concatenate(
                    [query * chosen[(g % 2) * per + c] for c in range(per)], axis=0
                )
                scores.append(
                    lax.dot_general(
                        keys[i * cluster : (i + 1) * cluster, band : band + LANES],
                        stacked, turned, preferred_element_type=f32,
                    )
                )
        weights = []
        for i in range(count):
            for g in range(HEADS // per):
                score = scores[i * (HEADS // per) + g]
                columns = pl.ds(g * per * cluster, per * cluster)
                top = jnp.max(score, axis=0, keepdims=True)
                weight = jnp.exp2(score - top)
                parts[places[i], head_width : head_width + 1, columns] = top
                parts[places[i], head_width + 1 : head_width + 2, columns] = jnp.sum(
                    weight, axis=0, keepdims=True
                )
                weights.append(weight.astype(bf16))
        for i in range(count):
            for g in range(HEADS // per):
                rows = per * head_width
                result = jnp.dot(
                    values[i][g * rows : (g + 1) * rows], weights[i * (HEADS // per) + g],
                    preferred_element_type=f32,
                )
                for k in range(per // 2):
                    top = 2 * k * head_width
                    lanes = slice(k * LANES, (k + 1) * LANES)
                    first = (g * per // 2 + k) * LANES
                    parts[places[i], 0:head_width, pl.ds(first, LANES)] = jnp.where(
                        low,
                        result[top : top + head_width, lanes],
                        result[top + head_width : top + 2 * head_width, lanes],
                    )

    def own_blocks(first, count, batch):
        def one(i, carry):
            index = [first + i * batch + k for k in range(batch)]
            several(index, [queries[j] for j in index], [blocks_ref[j] for j in index])
            return carry

        lax.fori_loop(0, count // batch, one, 0)

    def listed(which, source):
        batch = 5 if cap % 5 == 0 else 1

        def one(i, carry):
            index = [which * cap + i * batch + k for k in range(batch)]
            several(
                [block_count + j for j in index],
                [queries[reader_ref[j]] for j in index],
                [source[key_ref[j]] for j in index],
            )
            return carry

        lax.fori_loop(0, cap // batch, one, 0)

    def on_inner(work):
        pl.when(inner == 1)(work)

    def on_outer(work):
        pl.when(inner == 0)(work)

    def relay(s, c):
        far_copy(s, c).wait_recv()
        forward_copy(s, c).start()

    def refine(s):
        far_copy(s, 2).wait_recv()
        gather(4 + s, 0, cap, far[s], out_side, s * cap)
        filtered(s).start()

    def pass_on(s):
        far_copy(s, 0).wait_recv()
        passed_on(s).start()

    own_blocks(0, block_count // 2, 4)

    @pl.when(inner == 0)
    def _():
        for c in range(3):
            send_far(1, c)

    on_inner(lambda: relay(0, 0))
    own_blocks(block_count // 2, block_count // 2, 4)
    on_inner(lambda: relay(0, 1))
    listed(0, blocks_ref)
    near_copy(1).wait_recv()
    listed(1, near1)
    near_copy(2).wait_recv()
    listed(2, near2)
    near_copy(3).wait_recv()
    listed(3, near3)
    on_inner(lambda: refine(0))
    on_inner(lambda: relay(1, 0))
    on_outer(lambda: pass_on(0))
    on_outer(lambda: far_copy(0, 1).wait_recv())
    listed(4, far0)
    on_inner(lambda: relay(1, 1))
    on_outer(lambda: pass_on(1))
    filtered(0).wait_recv()
    listed(6, side0)
    on_inner(lambda: refine(1))

    @pl.when(inner == 1)
    def _():
        listed(5, far1)
        filtered(1).wait_recv()
        listed(7, side1)

    @pl.when(inner == 0)
    def _():
        filtered(1).wait_recv()
        listed(7, side1)
        far_copy(1, 1).wait_recv()
        listed(5, far1)

    def combine(i, carry):
        for k in range(SPAN):
            j = i * SPAN + k
            places = [j] + [slot_ref[j * pair_count + p] for p in range(pair_count)]
            tops = [parts[a, head_width : head_width + 1, :] for a in places]
            sums = [parts[a, head_width + 1 : head_width + 2, :] for a in places]
            top = functools.reduce(jnp.maximum, tops)
            factors = [jnp.exp2(t - top) for t in tops]
            total = sum(f * s for f, s in zip(factors, sums))
            inverse = 1.0 / total
            merged = sum(
                parts[a, 0:head_width, :] * (f * inverse) for a, f in zip(places, factors)
            ).astype(bf16)
            stacked = jnp.concatenate(
                [merged[:, c : c + LANES] for c in range(0, HEADS * cluster, LANES)], axis=0
            )
            upright = lax.dot_general(
                unit(LANES), stacked, turned, preferred_element_type=f32
            ).astype(bf16)
            rows = slice(k * cluster, (k + 1) * cluster)
            attended[rows, 0:LANES] = upright[0:cluster]
            attended[rows, LANES : 2 * LANES] = upright[cluster : 2 * cluster]
        here = pl.ds(pl.multiple_of(i * SPAN * cluster, SPAN * cluster), SPAN * cluster)
        projected = jnp.dot(attended[...], wo_sorted[...], preferred_element_type=f32)
        middle = (placed_ref[here, :].astype(f32) + projected).astype(bf16).astype(f32)
        second = layer_norm(middle).astype(bf16)
        mixed = middle + jnp.tanh(jnp.dot(second, wm_ref[...], preferred_element_type=f32))
        out_ref[here, :] = mixed.astype(bf16)
        return carry

    lax.fori_loop(0, block_count // SPAN, combine, 0)

    @pl.when(inner == 1)
    def _():
        for s in range(2):
            for c in range(2):
                forward_copy(s, c).wait_send()
            filtered(s).wait_send()

    @pl.when(inner == 0)
    def _():
        for s in range(2):
            passed_on(s).wait_send()

    for c in range(3):
        far_copy(0, c).wait_send()
    for t in range(1, 4):
        near_copy(t).wait_send()


def body(features, assignment, pairs, w_query, w_key, w_value, w_out, w_mix):
    rows_dev, width = features.shape
    block_count, pair_count = pairs.shape
    cluster = rows_dev // block_count
    capacity = (block_count * pair_count + SPAN - 1) // SPAN + 1
    stride = lax.axis_size("elec") // SPAN
    position = lax.axis_index("elec") // stride
    group_rows = SPAN * cluster
    groups = rows_dev // group_rows
    bf16 = jnp.bfloat16

    column, need = own_needs(pairs, block_count, stride)
    need_rows = SPAN * block_count // LANES
    batch = math.gcd(groups, 2)
    tile = pl.BlockSpec((batch * group_rows, width), lambda i: (i, 0))
    placed, normed, needs = pl.pallas_call(
        functools.partial(place_kernel, stride),
        grid=(groups // batch,),
        in_specs=[
            pl.BlockSpec((batch, 1, group_rows), lambda i: (i, 0, 0)),
            pl.BlockSpec((need_rows, LANES), lambda i: (0, 0)),
            tile,
        ],
        out_specs=[tile, tile, pl.BlockSpec((SPAN, need_rows, LANES), lambda i: (0, 0, 0))],
        out_shape=[jax.ShapeDtypeStruct((rows_dev, width), bf16)] * 2
        + [jax.ShapeDtypeStruct((SPAN, need_rows, LANES), jnp.int32)],
        scratch_shapes=[
            pltpu.VMEM((SPAN, need_rows, LANES), jnp.int32),
            pltpu.SemaphoreType.DMA((SPAN,)),
            pltpu.SemaphoreType.DMA((SPAN,)),
        ],
        compiler_params=pltpu.CompilerParams(collective_id=1, has_side_effects=True),
    )(
        assignment.reshape(groups, 1, group_rows), need.reshape(need_rows, LANES), features
    )

    tables, reader, key, slot = make_plan(
        needs.reshape(SPAN, SPAN, block_count), column, position, capacity, pair_count
    )
    block = (cluster, width)
    part = (head_step(width), HEADS * cluster)
    in_smem = pl.BlockSpec(memory_space=pltpu.SMEM)
    in_vmem = pl.BlockSpec(memory_space=pltpu.VMEM)
    return pl.pallas_call(
        functools.partial(layer_kernel, capacity, stride, pair_count),
        in_specs=[in_smem] * 4 + [in_vmem] * 7,
        out_specs=in_vmem,
        out_shape=jax.ShapeDtypeStruct((rows_dev, width), bf16),
        scratch_shapes=[pltpu.VMEM((capacity,) + block, bf16)] * 3
        + [pltpu.VMEM((block_count,) + block, bf16)] * 2
        + [pltpu.VMEM((capacity,) + block, bf16)] * 2
        + [
            pltpu.VMEM((3 * capacity,) + block, bf16),
            pltpu.VMEM((block_count,) + block, bf16),
            pltpu.VMEM((2 * capacity,) + block, bf16),
            pltpu.VMEM((block_count,) + block, bf16),
            pltpu.VMEM((width, width), bf16),
            pltpu.VMEM((width, width), bf16),
            pltpu.VMEM((block_count + SPAN * capacity,) + part, jnp.float32),
            pltpu.VMEM((SPAN * cluster, width), bf16),
            pltpu.SemaphoreType.DMA((3,)),
            pltpu.SemaphoreType.DMA((3,)),
            pltpu.SemaphoreType.DMA((3,)),
            pltpu.SemaphoreType.DMA((2, 2)),
            pltpu.SemaphoreType.DMA((2, 3)),
            pltpu.SemaphoreType.DMA((2,)),
            pltpu.SemaphoreType.DMA((2,)),
        ],
        compiler_params=pltpu.CompilerParams(
            collective_id=0, has_side_effects=True, vmem_limit_bytes=60 * 2**20
        ),
    )(
        tables, reader, key, slot, normed.reshape(block_count, cluster, width), placed,
        w_query, w_key, w_value, w_out, w_mix,
    )


def solution(mesh):
    placed = (
        P(("groups", "elec"), None),
        P(("groups", "elec")),
        P(("groups", "elec"), None),
        P(),
        P(),
        P(),
        P(),
        P(),
    )
    return jax.shard_map(
        body, mesh=mesh, in_specs=placed, out_specs=P(("groups", "elec"), None), check_vma=False
    )
```

time: 192 us -> 176 us (0.917)
  Pallas kernels: 182 us -> 165 us
    pallas_call x2 -> x1, Pallas kernels: 173 us -> 156 us  [body(): pl.pallas_call(functools.partial(layer_kernel, capacity, stride, pair_cou...]
    unnamed x19 -> x2, local copies, waits for them, and re-layouts: 5.89 us -> 3.82 us
where the time goes in v2:
time: 176 us; the launch traced here: 174 us
  Pallas kernels  165 us (94%)
  local copies, waits for them, and re-layouts  5.53 us (3%)
  other arithmetic  3.02 us (2%)
    pallas_call x1, Pallas kernels, body(): pl.pallas_call(functools.partial(layer_kernel, capacity, stride, pair_cou...  156 us
    pallas_call x1, Pallas kernels, body(): pl.pallas_call(functools.partial(place_kernel, stride), grid=(groups // b...  8.78 us
    unnamed x2, local copies, waits for them, and re-layouts  3.82 us

profile of v2, /device:TPU:12, one launch (start us, length us, event | category | flops | bytes accessed | tf_op | source)
XLA Modules:
  0.0 173.9 jit_solution(2672731097296196382)
XLA Ops:
  0.0 0.8 copy.10
  0.8 0.1 reshape.356
  1.0 0.7 select_reduce_fusion.1
  1.7 8.8 %shard_map.82 = (bf16[4096,256]{1,0:T(8,128)(2,1)}, bf16[4096,256]{1,0:T(8,128)(2,1)}, s32[8,4,128]{2,1,0:T(4,128)}) custom-call(s32[8,1,512]{2,1,0:T(1,128)} %bitcast.77, s32[4,128]{1,0:T(4,128)} %bitcast.78, bf16[4096,256]{1,0:T(8,128)(2,1)} %features_ref.1), custom_call_target="tpu_custom_call" | custom-call | tf_op jit(solution)/shard_map/pallas_call | solution.py:513
  10.5 0.8 reshape_reshape.3
  11.3 0.1 convolution_convert_fusion
  11.5 0.1 select_reduce_fusion.9
  11.6 0.1 select_reduce_fusion.7
  11.7 0.1 fusion.18
  11.9 0.1 fusion
  12.0 0.1 fusion.3
  12.1 0.2 fusion.14
  12.3 0.1 broadcast_in_dim.185
  12.4 0.2 select_reduce_fusion
  12.6 0.1 select_reduce_fusion.4
  12.7 0.1 select_reduce_fusion.6
  12.8 0.6 concatenate.3.tables_ref
  13.5 0.2 select_reduce_fusion.3
  13.6 0.5 broadcast_add_fusion
  14.2 0.1 select_reduce_fusion.2
  14.3 0.6 and_select_fusion
  14.9 155.9 %shard_map.83 = bf16[4096,256]{1,0:T(8,128)(2,1)} custom-call(s32[6,128]{1,0:T(8,128)} %concatenate.3.tables_ref, s32[200]{0:T(256)} %get-tuple-element.45.reader_ref, s32[200]{0:T(256)} %get-tuple-element.44.key_ref, s32[192]{0:T(256)} %get-tuple-element.13.slot_ref, bf16[64,64,256]{2,1,0:T(8,128)(2,1)} %bitcast.76, ...), custom_call_target="tpu_custom_call" | custom-call | tf_op jit(solution)/shard_map/pallas_call | solution.py:541
  170.8 3.0 %copy.12 = bf16[4096,256]{1,0:T(8,128)(2,1)} copy(bf16[4096,256]{1,0:T(8,128)(2,1)} %shard_map.83) | data formatting | bytes 4194304
  (12 shorter events, 0.2 us)

commit v3 on v2

--- a/solution.py
+++ b/solution.py
@@ -212,7 +212,10 @@
     near_devices = [device(z, pair_y), device(pair_z, y), device(pair_z, pair_y)]
     far_inner = device(2 - half, y)
     near, far, side = [near1, near2, near3], [far0, far1], [side0, side1]
-    chunks = [(0, cap), (cap, cap), (2 * cap, block_count - 2 * cap)]
+    first_half = (cap + 1) // 2
+    bounds = [0, first_half, cap, cap + first_half, 2 * cap, block_count]
+    chunks = [(a, b - a) for a, b in zip(bounds, bounds[1:])]
+    last = len(chunks) - 1
 
     barrier = pltpu.get_barrier_semaphore()
     for step in range(1, SPAN):
@@ -245,17 +248,19 @@
             device_id=near_devices[1], device_id_type=MESH,
         )
 
-    def side_copy(s, source):
+    def side_copy(s, k, source, base):
+        start, count = chunks[k]
         return pltpu.make_async_remote_copy(
-            src_ref=source, dst_ref=side[s], send_sem=p_send.at[s], recv_sem=p_recv.at[s],
+            src_ref=source.at[pl.ds(base + start, count)], dst_ref=side[s].at[pl.ds(start, count)],
+            send_sem=p_send.at[s, k], recv_sem=p_recv.at[s, k],
             device_id=near_devices[0], device_id_type=MESH,
         )
 
-    def filtered(s):
-        return side_copy(s, out_side.at[pl.ds(s * cap, cap)])
-
-    def passed_on(s):
-        return side_copy(s, far[s].at[pl.ds(0, cap)])
+    def filtered(s, k):
+        return side_copy(s, k, out_side, s * cap)
+
+    def passed_on(s, k):
+        return side_copy(s, k, far[s], 0)
 
     def near_copy(t):
         return pltpu.make_async_remote_copy(
@@ -274,8 +279,13 @@
 
     @pl.when(inner == 1)
     def _():
-        for c in range(3):
+        for c in range(last + 1):
             send_far(0, c)
+
+    @pl.when(inner == 0)
+    def _():
+        for c in range(last + 1):
+            send_far(1, c)
 
     for t in (2, 3, 1):
         send_near(t)
@@ -396,54 +406,72 @@
         forward_copy(s, c).start()
 
     def refine(s):
-        far_copy(s, 2).wait_recv()
+        far_copy(s, last).wait_recv()
         gather(4 + s, 0, cap, far[s], out_side, s * cap)
-        filtered(s).start()
-
-    def pass_on(s):
-        far_copy(s, 0).wait_recv()
-        passed_on(s).start()
-
-    own_blocks(0, block_count // 2, 4)
-
-    @pl.when(inner == 0)
-    def _():
-        for c in range(3):
-            send_far(1, c)
-
-    on_inner(lambda: relay(0, 0))
-    own_blocks(block_count // 2, block_count // 2, 4)
-    on_inner(lambda: relay(0, 1))
+        for k in range(2):
+            filtered(s, k).start()
+
+    def pass_on(s, k):
+        far_copy(s, k).wait_recv()
+        passed_on(s, k).start()
+
+    def arrived(s, first, stop):
+        for c in range(first, stop):
+            far_copy(s, c).wait_recv()
+
+    def side_arrived(s):
+        for k in range(2):
+            filtered(s, k).wait_recv()
+
+    eighth = block_count // 8
+    own_blocks(0, 3 * eighth, 4)
+    on_inner(lambda: relay(1, 0))
+    own_blocks(3 * eighth, 3 * eighth, 4)
+    on_inner(lambda: relay(1, 1))
+    own_blocks(6 * eighth, 2 * eighth, 4)
+    on_inner(lambda: relay(1, 2))
     listed(0, blocks_ref)
+    on_inner(lambda: relay(1, 3))
     near_copy(1).wait_recv()
     listed(1, near1)
-    near_copy(2).wait_recv()
-    listed(2, near2)
-    near_copy(3).wait_recv()
-    listed(3, near3)
-    on_inner(lambda: refine(0))
-    on_inner(lambda: relay(1, 0))
-    on_outer(lambda: pass_on(0))
-    on_outer(lambda: far_copy(0, 1).wait_recv())
-    listed(4, far0)
-    on_inner(lambda: relay(1, 1))
-    on_outer(lambda: pass_on(1))
-    filtered(0).wait_recv()
-    listed(6, side0)
     on_inner(lambda: refine(1))
 
     @pl.when(inner == 1)
     def _():
         listed(5, far1)
-        filtered(1).wait_recv()
+        relay(0, 0)
+        side_arrived(1)
         listed(7, side1)
+        relay(0, 1)
+        near_copy(2).wait_recv()
+        listed(2, near2)
+        relay(0, 2)
+        near_copy(3).wait_recv()
+        relay(0, 3)
+        refine(0)
+        listed(3, near3)
+        listed(4, far0)
+        side_arrived(0)
+        listed(6, side0)
 
     @pl.when(inner == 0)
     def _():
-        filtered(1).wait_recv()
+        pass_on(1, 0)
+        pass_on(1, 1)
+        near_copy(2).wait_recv()
+        listed(2, near2)
+        near_copy(3).wait_recv()
+        listed(3, near3)
+        arrived(1, 2, 4)
+        listed(5, far1)
+        side_arrived(1)
         listed(7, side1)
-        far_copy(1, 1).wait_recv()
-        listed(5, far1)
+        pass_on(0, 0)
+        pass_on(0, 1)
+        side_arrived(0)
+        listed(6, side0)
+        arrived(0, 2, 4)
+        listed(4, far0)
 
     def combine(i, carry):
         for k in range(SPAN):
@@ -480,16 +508,18 @@
     @pl.when(inner == 1)
     def _():
         for s in range(2):
-            for c in range(2):
+            for c in range(last):
                 forward_copy(s, c).wait_send()
-            filtered(s).wait_send()
+            for k in range(2):
+                filtered(s, k).wait_send()
 
     @pl.when(inner == 0)
     def _():
         for s in range(2):
-            passed_on(s).wait_send()
-
-    for c in range(3):
+            for k in range(2):
+                passed_on(s, k).wait_send()
+
+    for c in range(last + 1):
         far_copy(0, c).wait_send()
     for t in range(1, 4):
         near_copy(t).wait_send()
@@ -557,11 +587,11 @@
             pltpu.VMEM((SPAN * cluster, width), bf16),
             pltpu.SemaphoreType.DMA((3,)),
             pltpu.SemaphoreType.DMA((3,)),
-            pltpu.SemaphoreType.DMA((3,)),
+            pltpu.SemaphoreType.DMA((5,)),
+            pltpu.SemaphoreType.DMA((2, 4)),
+            pltpu.SemaphoreType.DMA((2, 5)),
             pltpu.SemaphoreType.DMA((2, 2)),
-            pltpu.SemaphoreType.DMA((2, 3)),
-            pltpu.SemaphoreType.DMA((2,)),
-            pltpu.SemaphoreType.DMA((2,)),
+            pltpu.SemaphoreType.DMA((2, 2)),
         ],
         compiler_params=pltpu.CompilerParams(
             collective_id=0, has_side_effects=True, vmem_limit_bytes=60 * 2**20

time: 176 us -> 149 us (0.85)
  Pallas kernels: 165 us -> 137 us
    pallas_call x1, Pallas kernels: 156 us -> 128 us  [body(): pl.pallas_call(functools.partial(layer_kernel, capacity, stride, pair_cou...]
where the time goes in v3:
time: 149 us; the launch traced here: 146 us
  Pallas kernels  137 us (92%)
  local copies, waits for them, and re-layouts  5.53 us (4%)
  other arithmetic  3.02 us (2%)
    pallas_call x1, Pallas kernels, body(): pl.pallas_call(functools.partial(layer_kernel, capacity, stride, pair_cou...  128 us
    pallas_call x1, Pallas kernels, body(): pl.pallas_call(functools.partial(place_kernel, stride), grid=(groups // b...  8.78 us
    unnamed x2, local copies, waits for them, and re-layouts  3.82 us

profile of v3, /device:TPU:12, one launch (start us, length us, event | category | flops | bytes accessed | tf_op | source)
XLA Modules:
  0.0 146.2 jit_solution(5690900482537563509)
XLA Ops:
  0.0 0.8 copy.10
  0.8 0.1 reshape.356
  1.0 0.7 select_reduce_fusion.1
  1.7 8.8 %shard_map.82 = (bf16[4096,256]{1,0:T(8,128)(2,1)}, bf16[4096,256]{1,0:T(8,128)(2,1)}, s32[8,4,128]{2,1,0:T(4,128)}) custom-call(s32[8,1,512]{2,1,0:T(1,128)} %bitcast.77, s32[4,128]{1,0:T(4,128)} %bitcast.78, bf16[4096,256]{1,0:T(8,128)(2,1)} %features_ref.1), custom_call_target="tpu_custom_call" | custom-call | tf_op jit(solution)/shard_map/pallas_call | solution.py:543
  10.5 0.8 reshape_reshape.3
  11.3 0.1 convolution_convert_fusion
  11.5 0.1 select_reduce_fusion.9
  11.6 0.1 select_reduce_fusion.7
  11.7 0.1 fusion.18
  11.9 0.1 fusion
  12.0 0.1 fusion.3
  12.1 0.2 fusion.14
  12.3 0.1 broadcast_in_dim.185
  12.4 0.2 select_reduce_fusion
  12.6 0.1 select_reduce_fusion.4
  12.7 0.1 select_reduce_fusion.6
  12.8 0.6 concatenate.3.tables_ref
  13.5 0.2 select_reduce_fusion.3
  13.6 0.5 broadcast_add_fusion
  14.2 0.1 select_reduce_fusion.2
  14.3 0.6 and_select_fusion
  14.9 128.3 %shard_map.83 = bf16[4096,256]{1,0:T(8,128)(2,1)} custom-call(s32[6,128]{1,0:T(8,128)} %concatenate.3.tables_ref, s32[200]{0:T(256)} %get-tuple-element.45.reader_ref, s32[200]{0:T(256)} %get-tuple-element.44.key_ref, s32[192]{0:T(256)} %get-tuple-element.13.slot_ref, bf16[64,64,256]{2,1,0:T(8,128)(2,1)} %bitcast.76, ...), custom_call_target="tpu_custom_call" | custom-call | tf_op jit(solution)/shard_map/pallas_call | solution.py:571
  143.2 3.0 %copy.12 = bf16[4096,256]{1,0:T(8,128)(2,1)} copy(bf16[4096,256]{1,0:T(8,128)(2,1)} %shard_map.83) | data formatting | bytes 4194304
  (12 shorter events, 0.2 us)

commit v4 on v3

--- a/solution.py
+++ b/solution.py
@@ -49,14 +49,27 @@
     blocks = needs.shape[-1]
     owners = jnp.arange(SPAN, dtype=jnp.int32)
     static = list(range(SPAN))
-    ends = [2 * (3 * (1 - o // 4)) + o % 2 for o in static]
-    first = jnp.stack([needs[ends[o] ^ 1, o] for o in static])
-    second = jnp.stack([needs[ends[o], o] for o in static]) * (1 - first)
-    third = 1 - first - second
-    c0, c1, c2 = before(first), before(second), before(third)
-    n0 = jnp.sum(first, axis=1, keepdims=True)
-    n1 = jnp.sum(second, axis=1, keepdims=True)
-    order = jnp.where(first > 0, c0, jnp.where(second > 0, n0 + c1, n0 + n1 + c2))
+
+    def arrange(*readers):
+        flags, left = [], jnp.ones((SPAN, blocks), jnp.int32)
+        for chosen in readers:
+            flags.append(jnp.stack([needs[chosen(o), o] for o in static]) * left)
+            left = left - flags[-1]
+        flags = jnp.stack(flags + [left])
+        counts = jnp.sum(flags, axis=-1, keepdims=True)
+        start = jnp.cumsum(counts, axis=0) - counts
+        return jnp.sum(flags * (before(flags) + start), axis=0)
+
+    def end(o):
+        return 2 * (3 * (1 - o // 4)) + o % 2
+
+    def middle(o):
+        return 2 * (2 - o // 4) + o % 2
+
+    order = arrange(
+        lambda o: end(o) ^ 1, end, lambda o: middle(o) ^ 1, middle
+    )
+    near_order = arrange(lambda o: o ^ 3, lambda o: o ^ 2)
     rank = before(needs)
     within = jnp.arange(blocks, dtype=jnp.int32)
 
@@ -65,14 +78,14 @@
 
     mine = lax.dynamic_index_in_dim(needs, position, 1, keepdims=False)
     mine_rank = lax.dynamic_index_in_dim(rank, position, 1, keepdims=False)
-    near = jnp.stack(
+    all_flags = jnp.ones((blocks,), jnp.int32)
+    lists = jnp.stack(
         [
-            invert(at(mine_rank, position ^ t), at(mine, position ^ t), within, LANES)
-            for t in range(1, 4)
+            invert(at(mine_rank, position ^ 1), at(mine, position ^ 1), within, LANES),
+            invert(at(near_order, position), all_flags, within, LANES),
+            invert(at(order, position), all_flags, within, LANES),
         ]
     )
-    all_flags = jnp.ones((blocks,), jnp.int32)
-    far_list = invert(at(order, position), all_flags, within, LANES)
 
     z, y = position // 2, position % 2
     half = z // 2
@@ -86,7 +99,7 @@
             for s in sources
         ]
     )
-    tables = jnp.concatenate([near, far_list[None], filters], axis=0)
+    tables = jnp.concatenate([lists, filters], axis=0)
 
     my_rank = at(rank, position)
     oz = owners // 2
@@ -96,11 +109,12 @@
     source_group = jnp.where(
         same_half, owners ^ position, jnp.where(same_line, 4 + outer_owner, 6 + outer_owner)
     )
+    by_rank = (owners == (position ^ 1)) | (~same_half & ~same_line & (inner > 0))
     location = jnp.where(
         (owners == position)[:, None],
         within[None, :],
         jnp.where(
-            same_half[:, None] | ((inner > 0) & ~same_line)[:, None], my_rank, order
+            by_rank[:, None], my_rank, jnp.where(same_half[:, None], near_order, order)
         ),
     )
     hit = column[:, None] == jnp.arange(SPAN * blocks, dtype=jnp.int32)[None, :]
@@ -128,9 +142,31 @@
     return -(-(width // HEADS + 2) // 8) * 8
 
 
+def excess(readers, limits):
+    rows = lax.broadcasted_iota(jnp.int32, readers[0].shape, 0)
+    lanes = lax.broadcasted_iota(jnp.int32, readers[0].shape, 1)
+    left = lanes < LANES // 2
+    lower = rows < SPAN // 4
+    large = jnp.maximum
+    end = jnp.where(lower, large(readers[6], readers[7]), large(readers[0], readers[1]))
+    middle = [jnp.where(lower, readers[4 + k], readers[2 + k]) for k in range(2)]
+    first = large(end, jnp.where(left, middle[1], middle[0]))
+    union = large(end, large(*middle))
+    near = large(readers[4], readers[5])
+    for row, k in ((0, 2), (1, 0), (2, 6)):
+        near = jnp.where(rows == row, large(readers[k], readers[k + 1]), near)
+    over = None
+    for flags, limit in zip((near, end, first, union), limits):
+        for part in (left, ~left):
+            count = jnp.sum(jnp.where(part, flags, 0).astype(jnp.float32), axis=1, keepdims=True)
+            worst = jnp.max(count, axis=0, keepdims=True) - float(limit)
+            over = worst if over is None else jnp.maximum(over, worst)
+    return over
+
+
 def place_kernel(
-    stride, assignment_ref, need_ref, features_ref, placed_ref, normed_ref, needs_ref,
-    landing, s_send, s_recv,
+    stride, limits, assignment_ref, need_ref, features_ref, placed_ref, normed_ref, needs_ref,
+    over_ref, landing, flags, s_send, s_recv, g_send, g_recv,
 ):
     groups, _, size = assignment_ref.shape
     me = lax.axis_index("elec")
@@ -138,9 +174,15 @@
     peers = lax.axis_size("elec")
     position = me // stride
     step_index = pl.program_id(0)
+    teams = flags.shape[0]
+    team = group * stride + lax.rem(me, stride)
 
     def toward(step):
         return (group, lax.rem(me + step * stride, peers))
+
+    def across(step):
+        other = lax.rem(team + step, teams)
+        return (other // stride, position * stride + lax.rem(other, stride))
 
     def ask(step):
         return pltpu.make_async_remote_copy(
@@ -149,15 +191,35 @@
             device_id=toward(step), device_id_type=MESH,
         )
 
+    def tell(step):
+        return pltpu.make_async_remote_copy(
+            src_ref=flags.at[0], dst_ref=flags.at[step],
+            send_sem=g_send.at[step], recv_sem=g_recv.at[step],
+            device_id=across(step), device_id_type=MESH,
+        )
+
     @pl.when(step_index == 0)
     def _():
         barrier = pltpu.get_barrier_semaphore()
         for step in range(1, SPAN):
             pl.semaphore_signal(barrier, inc=1, device_id=toward(step), device_id_type=MESH)
-        pl.semaphore_wait(barrier, SPAN - 1)
+        for step in range(1, teams):
+            pl.semaphore_signal(barrier, inc=1, device_id=across(step), device_id_type=MESH)
+        pl.semaphore_wait(barrier, SPAN - 1 + teams - 1)
         for step in range(1, SPAN):
             ask(step).start()
         landing[0] = need_ref[...]
+
+    @pl.when(step_index == pl.num_programs(0) // 2)
+    def _():
+        for step in range(1, SPAN):
+            ask(step).wait()
+        readers = [landing[lax.rem(position - q + SPAN, SPAN)] for q in range(SPAN)]
+        for q in range(SPAN):
+            needs_ref[q] = readers[q]
+        flags[0] = jnp.broadcast_to(excess(readers, limits), flags.shape[1:])
+        for step in range(1, teams):
+            tell(step).start()
 
     lane = lax.broadcasted_iota(jnp.int32, (size, LANES), 1).astype(jnp.float32)
     for i in range(groups):
@@ -176,19 +238,20 @@
 
     @pl.when(step_index == pl.num_programs(0) - 1)
     def _():
-        for step in range(1, SPAN):
-            ask(step).wait()
-        for q in range(SPAN):
-            needs_ref[q] = landing[lax.rem(position - q + SPAN, SPAN)]
+        for step in range(1, teams):
+            tell(step).wait()
+        worst = flags[0]
+        for step in range(1, teams):
+            worst = jnp.maximum(worst, flags[step])
+        over_ref[...] = worst
 
 
 def layer_kernel(
-    capacity, stride, pair_count,
-    tables_ref, reader_ref, key_ref, slot_ref,
-    blocks_ref, placed_ref, wq_ref, wk_ref, wv_ref, wo_ref, wm_ref,
+    capacity, limits, stride, pair_count,
+    tables_ref, reader_ref, key_ref, slot_ref, blocks_ref, wq_ref, wk_ref, wv_ref,
     out_ref,
-    near1, near2, near3, far0, far1, side0, side1, out_near, out_far, out_side,
-    queries, wv_turned, wo_sorted, parts, attended,
+    near1, near2, near3, far0, far1, rest0, rest1, side0, side1, out_near, out_plane, out_far, out_side,
+    queries, wv_turned, parts,
     n_send, n_recv, l_send, f_send, f_recv, p_send, p_recv,
 ):
     f32, bf16 = jnp.float32, jnp.bfloat16
@@ -211,11 +274,19 @@
 
     near_devices = [device(z, pair_y), device(pair_z, y), device(pair_z, pair_y)]
     far_inner = device(2 - half, y)
-    near, far, side = [near1, near2, near3], [far0, far1], [side0, side1]
-    first_half = (cap + 1) // 2
-    bounds = [0, first_half, cap, cap + first_half, 2 * cap, block_count]
+    far, late, side = [far0, far1], [rest0, rest1], [side0, side1]
+    near_limit, end_limit, first_limit, union_limit = limits
+    part_one = (cap + 1) // 2
+    part_two = cap + (end_limit - cap + 1) // 2
+    bounds = [0, part_one, cap, part_two, end_limit]
+    relayed = len(bounds) - 1
+    for bound in (first_limit, union_limit):
+        if bound > bounds[-1]:
+            bounds.append(bound)
     chunks = [(a, b - a) for a, b in zip(bounds, bounds[1:])]
     last = len(chunks) - 1
+    refinable = bounds.index(first_limit)
+    plane_chunks = [(0, cap), (cap, near_limit - cap)]
 
     barrier = pltpu.get_barrier_semaphore()
     for step in range(1, SPAN):
@@ -234,8 +305,11 @@
 
     def far_copy(s, c):
         start, count = chunks[c]
+        target = far[s].at[pl.ds(start, count)]
+        if c >= refinable:
+            target = late[s].at[pl.ds(start - first_limit, count)]
         return pltpu.make_async_remote_copy(
-            src_ref=out_far.at[pl.ds(start, count)], dst_ref=far[s].at[pl.ds(start, count)],
+            src_ref=out_far.at[pl.ds(start, count)], dst_ref=target,
             send_sem=l_send.at[c], recv_sem=f_recv.at[s, c],
             device_id=far_inner, device_id_type=MESH,
         )
@@ -262,19 +336,29 @@
     def passed_on(s, k):
         return side_copy(s, k, far[s], 0)
 
-    def near_copy(t):
+    def near_copy():
         return pltpu.make_async_remote_copy(
-            src_ref=out_near.at[pl.ds((t - 1) * cap, cap)], dst_ref=near[t - 1],
-            send_sem=n_send.at[t - 1], recv_sem=n_recv.at[t - 1],
-            device_id=near_devices[t - 1], device_id_type=MESH,
-        )
-
-    def send_near(t):
-        gather(t - 1, 0, cap, blocks_ref, out_near, (t - 1) * cap)
-        near_copy(t).start()
+            src_ref=out_near, dst_ref=near1, send_sem=n_send.at[0], recv_sem=n_recv.at[0],
+            device_id=near_devices[0], device_id_type=MESH,
+        )
+
+    def plane_copy(c):
+        start, count = plane_chunks[c]
+        return pltpu.make_async_remote_copy(
+            src_ref=out_plane.at[pl.ds(start, count)], dst_ref=near2.at[pl.ds(start, count)],
+            send_sem=n_send.at[1 + c], recv_sem=n_recv.at[1 + c],
+            device_id=near_devices[1], device_id_type=MESH,
+        )
+
+    def plane_pass():
+        return pltpu.make_async_remote_copy(
+            src_ref=near2.at[pl.ds(0, cap)], dst_ref=near3,
+            send_sem=n_send.at[3], recv_sem=n_recv.at[3],
+            device_id=near_devices[0], device_id_type=MESH,
+        )
 
     def send_far(s, c):
-        gather(3, chunks[c][0], chunks[c][1], blocks_ref, out_far, 0)
+        gather(2, chunks[c][0], chunks[c][1], blocks_ref, out_far, 0)
         far_copy(s, c).start()
 
     @pl.when(inner == 1)
@@ -284,11 +368,19 @@
 
     @pl.when(inner == 0)
     def _():
-        for c in range(last + 1):
+        for c in range(refinable):
             send_far(1, c)
 
-    for t in (2, 3, 1):
-        send_near(t)
+    gather(0, 0, cap, blocks_ref, out_near, 0)
+    near_copy().start()
+    for c in range(2):
+        gather(1, plane_chunks[c][0], plane_chunks[c][1], blocks_ref, out_plane, 0)
+        plane_copy(c).start()
+
+    @pl.when(inner == 0)
+    def _():
+        for c in range(refinable, last + 1):
+            send_far(1, c)
 
     lane = lax.broadcasted_iota(jnp.int32, (cluster, LANES), 1)
     per = LANES // 2 // head_width
@@ -307,11 +399,6 @@
     wv_turned[...] = lax.dot_general(
         unit(width), wv_ref[...], turned, preferred_element_type=f32
     ).astype(bf16)
-    for h in range(HEADS):
-        start = (h % 2) * (width // 2) + (h // 2) * head_width
-        wo_sorted[start : start + head_width, :] = wo_ref[
-            h * head_width : (h + 1) * head_width, :
-        ]
 
     def project(i, carry):
         rows = blocks_ref[pl.ds(i * SPAN, SPAN)].reshape(SPAN * cluster, width)
@@ -406,8 +493,8 @@
         forward_copy(s, c).start()
 
     def refine(s):
-        far_copy(s, last).wait_recv()
-        gather(4 + s, 0, cap, far[s], out_side, s * cap)
+        arrived(s, relayed, refinable)
+        gather(3 + s, 0, cap, far[s], out_side, s * cap)
         for k in range(2):
             filtered(s, k).start()
 
@@ -418,6 +505,11 @@
     def arrived(s, first, stop):
         for c in range(first, stop):
             far_copy(s, c).wait_recv()
+
+    def late_arrived(s):
+        arrived(s, refinable, last + 1)
+        for k in range(union_limit - first_limit):
+            far[s][first_limit + k] = late[s][k]
 
     def side_arrived(s):
         for k in range(2):
@@ -432,37 +524,43 @@
     on_inner(lambda: relay(1, 2))
     listed(0, blocks_ref)
     on_inner(lambda: relay(1, 3))
-    near_copy(1).wait_recv()
+    near_copy().wait_recv()
     listed(1, near1)
-    on_inner(lambda: refine(1))
 
     @pl.when(inner == 1)
     def _():
-        listed(5, far1)
+        refine(1)
         relay(0, 0)
+        plane_copy(0).wait_recv()
+        plane_pass().start()
+        relay(0, 1)
         side_arrived(1)
         listed(7, side1)
-        relay(0, 1)
-        near_copy(2).wait_recv()
+        relay(0, 2)
+        plane_copy(1).wait_recv()
+        relay(0, 3)
         listed(2, near2)
-        relay(0, 2)
-        near_copy(3).wait_recv()
-        relay(0, 3)
         refine(0)
+        late_arrived(1)
+        listed(5, far1)
+        plane_pass().wait_recv()
         listed(3, near3)
+        late_arrived(0)
         listed(4, far0)
         side_arrived(0)
         listed(6, side0)
 
     @pl.when(inner == 0)
     def _():
+        plane_copy(0).wait_recv()
+        plane_pass().start()
         pass_on(1, 0)
         pass_on(1, 1)
-        near_copy(2).wait_recv()
+        plane_copy(1).wait_recv()
         listed(2, near2)
-        near_copy(3).wait_recv()
+        plane_pass().wait_recv()
         listed(3, near3)
-        arrived(1, 2, 4)
+        arrived(1, 2, relayed)
         listed(5, far1)
         side_arrived(1)
         listed(7, side1)
@@ -470,7 +568,7 @@
         pass_on(0, 1)
         side_arrived(0)
         listed(6, side0)
-        arrived(0, 2, 4)
+        arrived(0, 2, relayed)
         listed(4, far0)
 
     def combine(i, carry):
@@ -492,15 +590,9 @@
             upright = lax.dot_general(
                 unit(LANES), stacked, turned, preferred_element_type=f32
             ).astype(bf16)
-            rows = slice(k * cluster, (k + 1) * cluster)
-            attended[rows, 0:LANES] = upright[0:cluster]
-            attended[rows, LANES : 2 * LANES] = upright[cluster : 2 * cluster]
-        here = pl.ds(pl.multiple_of(i * SPAN * cluster, SPAN * cluster), SPAN * cluster)
-        projected = jnp.dot(attended[...], wo_sorted[...], preferred_element_type=f32)
-        middle = (placed_ref[here, :].astype(f32) + projected).astype(bf16).astype(f32)
-        second = layer_norm(middle).astype(bf16)
-        mixed = middle + jnp.tanh(jnp.dot(second, wm_ref[...], preferred_element_type=f32))
-        out_ref[here, :] = mixed.astype(bf16)
+            rows = pl.ds(pl.multiple_of(j * cluster, cluster), cluster)
+            out_ref[rows, 0:LANES] = upright[0:cluster]
+            out_ref[rows, LANES : 2 * LANES] = upright[cluster : 2 * cluster]
         return carry
 
     lax.fori_loop(0, block_count // SPAN, combine, 0)
@@ -508,7 +600,7 @@
     @pl.when(inner == 1)
     def _():
         for s in range(2):
-            for c in range(last):
+            for c in range(relayed):
                 forward_copy(s, c).wait_send()
             for k in range(2):
                 filtered(s, k).wait_send()
@@ -521,8 +613,30 @@
 
     for c in range(last + 1):
         far_copy(0, c).wait_send()
-    for t in range(1, 4):
-        near_copy(t).wait_send()
+    near_copy().wait_send()
+    for c in range(2):
+        plane_copy(c).wait_send()
+    plane_pass().wait_send()
+
+
+def finish_kernel(placed_ref, attended_ref, wo_ref, wm_ref, out_ref, wo_sorted):
+    f32, bf16 = jnp.float32, jnp.bfloat16
+    width = wo_ref.shape[0]
+    head_width = width // HEADS
+
+    @pl.when(pl.program_id(0) == 0)
+    def _():
+        for h in range(HEADS):
+            start = (h % 2) * (width // 2) + (h // 2) * head_width
+            wo_sorted[start : start + head_width, :] = wo_ref[
+                h * head_width : (h + 1) * head_width, :
+            ]
+
+    projected = jnp.dot(attended_ref[...], wo_sorted[...], preferred_element_type=f32)
+    middle = (placed_ref[...].astype(f32) + projected).astype(bf16).astype(f32)
+    second = layer_norm(middle).astype(bf16)
+    mixed = middle + jnp.tanh(jnp.dot(second, wm_ref[...], preferred_element_type=f32))
+    out_ref[...] = mixed.astype(bf16)
 
 
 def body(features, assignment, pairs, w_query, w_key, w_value, w_out, w_mix):
@@ -540,21 +654,36 @@
     need_rows = SPAN * block_count // LANES
     batch = math.gcd(groups, 2)
     tile = pl.BlockSpec((batch * group_rows, width), lambda i: (i, 0))
-    placed, normed, needs = pl.pallas_call(
-        functools.partial(place_kernel, stride),
+    full = (2 * capacity, 2 * capacity, block_count, block_count)
+    small = (capacity + 18, capacity + 18, capacity + 27, capacity + 34)
+    limits = tuple(min(a, b) for a, b in zip(small, full))
+    teams = lax.axis_size("groups") * stride
+    placed, normed, needs, over = pl.pallas_call(
+        functools.partial(place_kernel, stride, limits),
         grid=(groups // batch,),
         in_specs=[
             pl.BlockSpec((batch, 1, group_rows), lambda i: (i, 0, 0)),
             pl.BlockSpec((need_rows, LANES), lambda i: (0, 0)),
             tile,
         ],
-        out_specs=[tile, tile, pl.BlockSpec((SPAN, need_rows, LANES), lambda i: (0, 0, 0))],
+        out_specs=[
+            tile,
+            tile,
+            pl.BlockSpec((SPAN, need_rows, LANES), lambda i: (0, 0, 0)),
+            pl.BlockSpec((8, LANES), lambda i: (0, 0)),
+        ],
         out_shape=[jax.ShapeDtypeStruct((rows_dev, width), bf16)] * 2
-        + [jax.ShapeDtypeStruct((SPAN, need_rows, LANES), jnp.int32)],
+        + [
+            jax.ShapeDtypeStruct((SPAN, need_rows, LANES), jnp.int32),
+            jax.ShapeDtypeStruct((8, LANES), jnp.float32),
+        ],
         scratch_shapes=[
             pltpu.VMEM((SPAN, need_rows, LANES), jnp.int32),
+            pltpu.VMEM((teams, 8, LANES), jnp.float32),
             pltpu.SemaphoreType.DMA((SPAN,)),
             pltpu.SemaphoreType.DMA((SPAN,)),
+            pltpu.SemaphoreType.DMA((teams,)),
+            pltpu.SemaphoreType.DMA((teams,)),
         ],
         compiler_params=pltpu.CompilerParams(collective_id=1, has_side_effects=True),
     )(
@@ -568,38 +697,53 @@
     part = (head_step(width), HEADS * cluster)
     in_smem = pl.BlockSpec(memory_space=pltpu.SMEM)
     in_vmem = pl.BlockSpec(memory_space=pltpu.VMEM)
+
+    def layer(which, sizes):
+        near_limit, end_limit, first_limit, union_limit = sizes
+        steps = 4 + len({end_limit, first_limit, union_limit}) - 1
+        buffers = [
+            capacity, near_limit, capacity, union_limit, union_limit,
+            max(union_limit - first_limit, 1), max(union_limit - first_limit, 1),
+            capacity, capacity,
+            capacity, near_limit, union_limit, 2 * capacity, block_count,
+        ]
+        return pl.pallas_call(
+            functools.partial(layer_kernel, capacity, sizes, stride, pair_count),
+            in_specs=[in_smem] * 4 + [in_vmem] * 4,
+            out_specs=in_vmem,
+            out_shape=jax.ShapeDtypeStruct((rows_dev, width), bf16),
+            scratch_shapes=[pltpu.VMEM((count,) + block, bf16) for count in buffers]
+            + [
+                pltpu.VMEM((width, width), bf16),
+                pltpu.VMEM((block_count + SPAN * capacity,) + part, jnp.float32),
+                pltpu.SemaphoreType.DMA((4,)),
+                pltpu.SemaphoreType.DMA((4,)),
+                pltpu.SemaphoreType.DMA((steps,)),
+                pltpu.SemaphoreType.DMA((2, 4)),
+                pltpu.SemaphoreType.DMA((2, steps)),
+                pltpu.SemaphoreType.DMA((2, 2)),
+                pltpu.SemaphoreType.DMA((2, 2)),
+            ],
+            compiler_params=pltpu.CompilerParams(
+                collective_id=which, has_side_effects=True, vmem_limit_bytes=60 * 2**20
+            ),
+        )
+
+    attended = lax.cond(
+        over[0, 0] <= 0.0, layer(0, limits), layer(2, full),
+        tables, reader, key, slot, normed.reshape(block_count, cluster, width),
+        w_query, w_key, w_value,
+    )
+    tile = pl.BlockSpec((group_rows, width), lambda i: (i, 0))
+    weight = pl.BlockSpec((width, width), lambda i: (0, 0))
     return pl.pallas_call(
-        functools.partial(layer_kernel, capacity, stride, pair_count),
-        in_specs=[in_smem] * 4 + [in_vmem] * 7,
-        out_specs=in_vmem,
+        finish_kernel,
+        grid=(groups,),
+        in_specs=[tile, tile, weight, weight],
+        out_specs=tile,
         out_shape=jax.ShapeDtypeStruct((rows_dev, width), bf16),
-        scratch_shapes=[pltpu.VMEM((capacity,) + block, bf16)] * 3
-        + [pltpu.VMEM((block_count,) + block, bf16)] * 2
-        + [pltpu.VMEM((capacity,) + block, bf16)] * 2
-        + [
-            pltpu.VMEM((3 * capacity,) + block, bf16),
-            pltpu.VMEM((block_count,) + block, bf16),
-            pltpu.VMEM((2 * capacity,) + block, bf16),
-            pltpu.VMEM((block_count,) + block, bf16),
-            pltpu.VMEM((width, width), bf16),
-            pltpu.VMEM((width, width), bf16),
-            pltpu.VMEM((block_count + SPAN * capacity,) + part, jnp.float32),
-            pltpu.VMEM((SPAN * cluster, width), bf16),
-            pltpu.SemaphoreType.DMA((3,)),
-            pltpu.SemaphoreType.DMA((3,)),
-            pltpu.SemaphoreType.DMA((5,)),
-            pltpu.SemaphoreType.DMA((2, 4)),
-            pltpu.SemaphoreType.DMA((2, 5)),
-            pltpu.SemaphoreType.DMA((2, 2)),
-            pltpu.SemaphoreType.DMA((2, 2)),
-        ],
-        compiler_params=pltpu.CompilerParams(
-            collective_id=0, has_side_effects=True, vmem_limit_bytes=60 * 2**20
-        ),
-    )(
-        tables, reader, key, slot, normed.reshape(block_count, cluster, width), placed,
-        w_query, w_key, w_value, w_out, w_mix,
-    )
+        scratch_shapes=[pltpu.VMEM((width, width), bf16)],
+    )(placed, attended, w_out, w_mix)
 
 
 def solution(mesh):

time: 149 us -> 141 us (0.946); the launches traced: 146 us -> 141 us
  Pallas kernels: 137 us -> 133 us
  local copies, waits for them, and re-layouts: 5.53 us -> 3.92 us
    pallas_call x2 -> x3, Pallas kernels: 137 us -> 133 us  [the longest x1 112 us: body(): lax.cond(over[0, 0] <= 0.0, layer(0, limits), layer(2, full), tables, rea...]
    unnamed x2 -> x8, local copies, waits for them, and re-layouts: 3.82 us -> 0.78 us
where the time goes in v4:
time: 141 us
  Pallas kernels  133 us (94%)
  local copies, waits for them, and re-layouts  3.92 us (3%)
  other arithmetic  2.4 us (2%)
    pallas_call x1, Pallas kernels, body(): lax.cond(over[0, 0] <= 0.0, layer(0, limits), layer(2, full), tables, rea...  112 us
    pallas_call x1, Pallas kernels, body(): pl.pallas_call(functools.partial(place_kernel, stride, limits), grid=(gro...  12 us
    pallas_call x1, Pallas kernels, body(): pl.pallas_call(finish_kernel, grid=(groups,), in_specs=[tile, tile, weigh...  8.3 us

profile of v4, /device:TPU:12, one launch (start us, length us, event | category | flops | bytes accessed | tf_op | source)
XLA Modules:
  0.0 140.9 jit_solution(7845080960359240944)
XLA Ops:
  0.0 0.0 copy-start.2
  0.0 0.0 copy-start.1
  0.0 0.0 copy-start
  0.2 0.1 broadcast_in_dim.180
  0.3 0.1 broadcast_in_dim.181
  0.4 0.1 broadcast_in_dim.176
  0.4 0.1 broadcast_in_dim.177
  0.5 0.1 broadcast_in_dim.174
  0.6 0.1 broadcast_in_dim.175
  0.7 0.1 broadcast_in_dim.179
  0.7 0.8 copy.10
  1.5 0.1 reshape.1667
  1.7 0.7 select_reduce_fusion.1
  2.4 12.0 %shard_map.82 = (bf16[4096,256]{1,0:T(8,128)(2,1)}, bf16[4096,256]{1,0:T(8,128)(2,1)}, s32[8,4,128]{2,1,0:T(4,128)}, f32[8,128]{1,0:T(8,128)}) custom-call(s32[8,1,512]{2,1,0:T(1,128)} %bitcast.71, s32[4,128]{1,0:T(4,128)} %bitcast.74, bf16[4096,256]{1,0:T(8,128)(2,1)} %features_ref.1), custom_call_target="tpu_custom_call" | custom-call | tf_op jit(solution)/shard_map/pallas_call | solution.py:661
  14.4 1.2 slice.147
  16.3 0.8 reshape_reshape.3
  17.3 0.1 convolution_convert_fusion
  17.4 0.1 squeeze.21
  17.5 0.1 select_reduce_fusion.8
  17.7 0.1 fusion.17
  17.9 0.1 fusion.5
  18.0 0.1 constant_dynamic-update-slice_fusion.3
  18.1 0.2 reduce_sum.112
  18.3 0.1 fusion.2
  18.5 0.1 broadcast_select_fusion
  18.6 0.1 select_n.295
  18.6 0.2 select_reduce_fusion
  18.8 0.1 select_reduce_fusion.5
  19.0 0.1 select_reduce_fusion.4
  19.1 0.1 select_reduce_fusion.6
  19.2 0.1 select_reduce_fusion.7
  19.3 0.2 select_reduce_fusion.3
  19.5 0.1 select_reduce_fusion.2
  19.6 0.0 copy-done.2
  19.7 0.0 copy-done.1
  19.7 0.0 copy-done
  19.7 112.9 %conditional.1 = (bf16[4096,256]{1,0:T(8,128)(2,1)S(1)}) conditional(s32[]{:T(128)} %bitcast.2, (s32[5,128]{1,0:T(8,128)S(1)}, s32[200]{0:T(256)S(1)}, s32[200]{0:T(256)S(1)}, s32[192]{0:T(256)S(1)}, bf16[64,64,256]{2,1,0:T(8,128)(2,1)}, /*index=5*/bf16[256,256]{1,0:T(8,128)(2,1)S(1)}, bf16[256,256]{1,0:T(8,128)(2,1)S(1)}, ...), branch_computations={%region_15.16_spmd, %region_16.17_spmd} | conditional | bytes 8 | solution.py:732
  19.9 112.4 %branch_1_fun.1 = bf16[4096,256]{1,0:T(8,128)(2,1)S(1)} custom-call(s32[5,128]{1,0:T(8,128)S(1)} %get-tuple-element.48.tables_ref, s32[200]{0:T(256)S(1)} %get-tuple-element.49.reader_ref, s32[200]{0:T(256)S(1)} %get-tuple-element.50.key_ref, s32[192]{0:T(256)S(1)} %get-tuple-element.51.slot_ref, bf16[64,64,256]{2,1,0:T(8,128)(2,1)} %get-tuple-element.52.blocks_ref, ...), custom_call_target="tpu_custom_call" | custom-call | tf_op jit(solution)/shard_map/cond/branch_1_fun/pallas_call | solution.py:732
  132.6 8.3 %shard_map.83 = bf16[4096,256]{1,0:T(8,128)(2,1)} custom-call(bf16[4096,256]{1,0:T(8,128)(2,1)} %get-tuple-element.60.placed_ref, bf16[4096,256]{1,0:T(8,128)(2,1)S(1)} %get-tuple-element.148.attended_ref, bf16[256,256]{1,0:T(8,128)(2,1)} %wo_ref.1, bf16[256,256]{1,0:T(8,128)(2,1)} %wm_ref.1), custom_call_target="tpu_custom_call" | custom-call | tf_op jit(solution)/shard_map/pallas_call | solution.py:739
  (35 shorter events, 0.5 us)
Async XLA Ops:
  0.0 19.7 %copy-start.2 = (bf16[256,256]{1,0:T(8,128)(2,1)S(1)}, bf16[256,256]{1,0:T(8,128)(2,1)}, u32[]{:S(2)}) copy-start(bf16[256,256]{1,0:T(8,128)(2,1)} %param.15) | copy-start | bytes 393220
  0.0 19.7 %copy-start.1 = (bf16[256,256]{1,0:T(8,128)(2,1)S(1)}, bf16[256,256]{1,0:T(8,128)(2,1)}, u32[]{:S(2)}) copy-start(bf16[256,256]{1,0:T(8,128)(2,1)} %param.14) | copy-start | bytes 393220
  0.0 19.7 %copy-start = (bf16[256,256]{1,0:T(8,128)(2,1)S(1)}, bf16[256,256]{1,0:T(8,128)(2,1)}, u32[]{:S(2)}) copy-start(bf16[256,256]{1,0:T(8,128)(2,1)} %param.13) | copy-start | bytes 393220

commit v5 on v4

--- a/solution.py
+++ b/solution.py
@@ -210,7 +210,7 @@
             ask(step).start()
         landing[0] = need_ref[...]
 
-    @pl.when(step_index == pl.num_programs(0) // 2)
+    @pl.when(step_index == pl.num_programs(0) - 1)
     def _():
         for step in range(1, SPAN):
             ask(step).wait()
@@ -243,7 +243,7 @@
         worst = flags[0]
         for step in range(1, teams):
             worst = jnp.maximum(worst, flags[step])
-        over_ref[...] = worst
+        over_ref[0, 0] = jnp.max(worst)
 
 
 def layer_kernel(
@@ -670,12 +670,12 @@
             tile,
             tile,
             pl.BlockSpec((SPAN, need_rows, LANES), lambda i: (0, 0, 0)),
-            pl.BlockSpec((8, LANES), lambda i: (0, 0)),
+            pl.BlockSpec(memory_space=pltpu.SMEM),
         ],
         out_shape=[jax.ShapeDtypeStruct((rows_dev, width), bf16)] * 2
         + [
             jax.ShapeDtypeStruct((SPAN, need_rows, LANES), jnp.int32),
-            jax.ShapeDtypeStruct((8, LANES), jnp.float32),
+            jax.ShapeDtypeStruct((1, 1), jnp.float32),
         ],
         scratch_shapes=[
             pltpu.VMEM((SPAN, need_rows, LANES), jnp.int32),
@@ -734,15 +734,17 @@
         tables, reader, key, slot, normed.reshape(block_count, cluster, width),
         w_query, w_key, w_value,
     )
-    tile = pl.BlockSpec((group_rows, width), lambda i: (i, 0))
+    finish_rows = math.gcd(groups, 4) * group_rows
+    tile = pl.BlockSpec((finish_rows, width), lambda i: (i, 0))
     weight = pl.BlockSpec((width, width), lambda i: (0, 0))
     return pl.pallas_call(
         finish_kernel,
-        grid=(groups,),
+        grid=(rows_dev // finish_rows,),
         in_specs=[tile, tile, weight, weight],
         out_specs=tile,
         out_shape=jax.ShapeDtypeStruct((rows_dev, width), bf16),
         scratch_shapes=[pltpu.VMEM((width, width), bf16)],
+        compiler_params=pltpu.CompilerParams(vmem_limit_bytes=60 * 2**20),
     )(placed, attended, w_out, w_mix)
 
 

time: 141 us -> 137 us (0.972)
  Pallas kernels: 133 us -> 130 us
    pallas_call x1, Pallas kernels: 8.3 us -> 5.12 us  [body(): pl.pallas_call(finish_kernel, grid=(rows_dev // finish_rows,), in_specs=[...]
where the time goes in v5:
time: 137 us
  Pallas kernels  130 us (95%)
  local copies, waits for them, and re-layouts  2.73 us (2%)
  other arithmetic  2.4 us (2%)
    pallas_call x1, Pallas kernels, body(): lax.cond(over[0, 0] <= 0.0, layer(0, limits), layer(2, full), tables, rea...  112 us
    pallas_call x1, Pallas kernels, body(): pl.pallas_call(functools.partial(place_kernel, stride, limits), grid=(gro...  12.2 us
    pallas_call x1, Pallas kernels, body(): pl.pallas_call(finish_kernel, grid=(rows_dev // finish_rows,), in_specs=[...  5.12 us

profile of v5, /device:TPU:12, one launch (start us, length us, event | category | flops | bytes accessed | tf_op | source)
XLA Modules:
  0.0 136.6 jit_solution(17712228881262052414)
XLA Ops:
  0.0 0.0 copy-start.2
  0.0 0.0 copy-start.1
  0.0 0.0 copy-start
  0.2 0.1 broadcast_in_dim.180
  0.3 0.1 broadcast_in_dim.181
  0.4 0.1 broadcast_in_dim.176
  0.4 0.1 broadcast_in_dim.177
  0.5 0.1 broadcast_in_dim.174
  0.6 0.1 broadcast_in_dim.175
  0.7 0.1 broadcast_in_dim.179
  0.7 0.8 copy.10
  1.5 0.1 reshape.1667
  1.7 0.7 select_reduce_fusion.1
  2.4 12.2 %shard_map.82 = (bf16[4096,256]{1,0:T(8,128)(2,1)}, bf16[4096,256]{1,0:T(8,128)(2,1)}, s32[8,4,128]{2,1,0:T(4,128)}, f32[1,1]{1,0:T(1,128)}) custom-call(s32[8,1,512]{2,1,0:T(1,128)} %bitcast.71, s32[4,128]{1,0:T(4,128)} %bitcast.74, bf16[4096,256]{1,0:T(8,128)(2,1)} %features_ref.1), custom_call_target="tpu_custom_call" | custom-call | tf_op jit(solution)/shard_map/pallas_call | solution.py:661
  15.2 0.8 reshape_reshape.3
  16.2 0.1 convolution_convert_fusion
  16.3 0.1 squeeze.21
  16.4 0.1 select_reduce_fusion.8
  16.6 0.1 fusion.17
  16.8 0.1 fusion.5
  16.9 0.1 constant_dynamic-update-slice_fusion.3
  17.0 0.2 reduce_sum.112
  17.2 0.1 fusion.2
  17.4 0.1 broadcast_select_fusion
  17.5 0.1 select_n.295
  17.5 0.2 select_reduce_fusion
  17.7 0.1 select_reduce_fusion.5
  17.8 0.1 select_reduce_fusion.4
  18.0 0.1 select_reduce_fusion.6
  18.1 0.1 select_reduce_fusion.7
  18.2 0.2 select_reduce_fusion.3
  18.4 0.1 select_reduce_fusion.2
  18.5 0.0 copy-done.2
  18.6 0.0 copy-done.1
  18.6 0.0 copy-done
  18.6 112.9 %conditional.1 = (bf16[4096,256]{1,0:T(8,128)(2,1)S(1)}) conditional(s32[]{:T(128)} %bitcast.2, (s32[5,128]{1,0:T(8,128)S(1)}, s32[200]{0:T(256)S(1)}, s32[200]{0:T(256)S(1)}, s32[192]{0:T(256)S(1)}, bf16[64,64,256]{2,1,0:T(8,128)(2,1)}, /*index=5*/bf16[256,256]{1,0:T(8,128)(2,1)S(1)}, bf16[256,256]{1,0:T(8,128)(2,1)S(1)}, ...), branch_computations={%region_15.16_spmd, %region_16.17_spmd} | conditional | bytes 8 | solution.py:732
  18.8 112.4 %branch_1_fun.1 = bf16[4096,256]{1,0:T(8,128)(2,1)S(1)} custom-call(s32[5,128]{1,0:T(8,128)S(1)} %get-tuple-element.48.tables_ref, s32[200]{0:T(256)S(1)} %get-tuple-element.49.reader_ref, s32[200]{0:T(256)S(1)} %get-tuple-element.50.key_ref, s32[192]{0:T(256)S(1)} %get-tuple-element.51.slot_ref, bf16[64,64,256]{2,1,0:T(8,128)(2,1)} %get-tuple-element.52.blocks_ref, ...), custom_call_target="tpu_custom_call" | custom-call | tf_op jit(solution)/shard_map/cond/branch_1_fun/pallas_call | solution.py:732
  131.5 5.1 %shard_map.83 = bf16[4096,256]{1,0:T(8,128)(2,1)} custom-call(bf16[4096,256]{1,0:T(8,128)(2,1)} %get-tuple-element.60.placed_ref, bf16[4096,256]{1,0:T(8,128)(2,1)S(1)} %get-tuple-element.148.attended_ref, bf16[256,256]{1,0:T(8,128)(2,1)} %wo_ref.1, bf16[256,256]{1,0:T(8,128)(2,1)} %wm_ref.1), custom_call_target="tpu_custom_call" | custom-call | tf_op jit(solution)/shard_map/pallas_call | solution.py:740
  (35 shorter events, 0.5 us)
Async XLA Ops:
  0.0 18.5 %copy-start.2 = (bf16[256,256]{1,0:T(8,128)(2,1)S(1)}, bf16[256,256]{1,0:T(8,128)(2,1)}, u32[]{:S(2)}) copy-start(bf16[256,256]{1,0:T(8,128)(2,1)} %param.15) | copy-start | bytes 393220
  0.0 18.6 %copy-start.1 = (bf16[256,256]{1,0:T(8,128)(2,1)S(1)}, bf16[256,256]{1,0:T(8,128)(2,1)}, u32[]{:S(2)}) copy-start(bf16[256,256]{1,0:T(8,128)(2,1)} %param.14) | copy-start | bytes 393220
  0.0 18.6 %copy-start = (bf16[256,256]{1,0:T(8,128)(2,1)S(1)}, bf16[256,256]{1,0:T(8,128)(2,1)}, u32[]{:S(2)}) copy-start(bf16[256,256]{1,0:T(8,128)(2,1)} %param.13) | copy-start | bytes 393220

commit v6 on v5

--- a/solution.py
+++ b/solution.py
@@ -376,11 +376,6 @@
     for c in range(2):
         gather(1, plane_chunks[c][0], plane_chunks[c][1], blocks_ref, out_plane, 0)
         plane_copy(c).start()
-
-    @pl.when(inner == 0)
-    def _():
-        for c in range(refinable, last + 1):
-            send_far(1, c)
 
     lane = lax.broadcasted_iota(jnp.int32, (cluster, LANES), 1)
     per = LANES // 2 // head_width
@@ -541,12 +536,12 @@
         relay(0, 3)
         listed(2, near2)
         refine(0)
-        late_arrived(1)
-        listed(5, far1)
         plane_pass().wait_recv()
         listed(3, near3)
         late_arrived(0)
         listed(4, far0)
+        late_arrived(1)
+        listed(5, far1)
         side_arrived(0)
         listed(6, side0)
 
@@ -565,6 +560,8 @@
         side_arrived(1)
         listed(7, side1)
         pass_on(0, 0)
+        for c in range(refinable, last + 1):
+            send_far(1, c)
         pass_on(0, 1)
         side_arrived(0)
         listed(6, side0)

time: 137 us -> 137 us (level)
  no operation moved by 1% of the time
where the time goes in v6:
time: 137 us
  Pallas kernels  130 us (95%)
  local copies, waits for them, and re-layouts  2.73 us (2%)
  other arithmetic  2.4 us (2%)
    pallas_call x1, Pallas kernels, body(): lax.cond(over[0, 0] <= 0.0, layer(0, limits), layer(2, full), tables, rea...  112 us
    pallas_call x1, Pallas kernels, body(): pl.pallas_call(functools.partial(place_kernel, stride, limits), grid=(gro...  12.2 us
    pallas_call x1, Pallas kernels, body(): pl.pallas_call(finish_kernel, grid=(rows_dev // finish_rows,), in_specs=[...  5.12 us

profile of v6, /device:TPU:12, one launch (start us, length us, event | category | flops | bytes accessed | tf_op | source)
XLA Modules:
  0.0 136.6 jit_solution(2622658612947886801)
XLA Ops:
  0.0 0.0 copy-start.2
  0.0 0.0 copy-start.1
  0.0 0.0 copy-start
  0.2 0.1 broadcast_in_dim.180
  0.3 0.1 broadcast_in_dim.181
  0.4 0.1 broadcast_in_dim.176
  0.4 0.1 broadcast_in_dim.177
  0.5 0.1 broadcast_in_dim.174
  0.6 0.1 broadcast_in_dim.175
  0.7 0.1 broadcast_in_dim.179
  0.7 0.8 copy.10
  1.5 0.1 reshape.1667
  1.7 0.7 select_reduce_fusion.1
  2.4 12.2 %shard_map.82 = (bf16[4096,256]{1,0:T(8,128)(2,1)}, bf16[4096,256]{1,0:T(8,128)(2,1)}, s32[8,4,128]{2,1,0:T(4,128)}, f32[1,1]{1,0:T(1,128)}) custom-call(s32[8,1,512]{2,1,0:T(1,128)} %bitcast.71, s32[4,128]{1,0:T(4,128)} %bitcast.74, bf16[4096,256]{1,0:T(8,128)(2,1)} %features_ref.1), custom_call_target="tpu_custom_call" | custom-call | tf_op jit(solution)/shard_map/pallas_call | solution.py:658
  15.2 0.8 reshape_reshape.3
  16.2 0.1 convolution_convert_fusion
  16.3 0.1 squeeze.21
  16.4 0.1 select_reduce_fusion.8
  16.6 0.1 fusion.17
  16.8 0.1 fusion.5
  16.9 0.1 constant_dynamic-update-slice_fusion.3
  17.0 0.2 reduce_sum.112
  17.2 0.1 fusion.2
  17.4 0.1 broadcast_select_fusion
  17.5 0.1 select_n.295
  17.5 0.2 select_reduce_fusion
  17.7 0.1 select_reduce_fusion.5
  17.8 0.1 select_reduce_fusion.4
  18.0 0.1 select_reduce_fusion.6
  18.1 0.1 select_reduce_fusion.7
  18.2 0.2 select_reduce_fusion.3
  18.4 0.1 select_reduce_fusion.2
  18.5 0.0 copy-done.2
  18.6 0.0 copy-done.1
  18.6 0.0 copy-done
  18.6 112.9 %conditional.1 = (bf16[4096,256]{1,0:T(8,128)(2,1)S(1)}) conditional(s32[]{:T(128)} %bitcast.2, (s32[5,128]{1,0:T(8,128)S(1)}, s32[200]{0:T(256)S(1)}, s32[200]{0:T(256)S(1)}, s32[192]{0:T(256)S(1)}, bf16[64,64,256]{2,1,0:T(8,128)(2,1)}, /*index=5*/bf16[256,256]{1,0:T(8,128)(2,1)S(1)}, bf16[256,256]{1,0:T(8,128)(2,1)S(1)}, ...), branch_computations={%region_15.16_spmd, %region_16.17_spmd} | conditional | bytes 8 | solution.py:729
  18.8 112.4 %branch_1_fun.1 = bf16[4096,256]{1,0:T(8,128)(2,1)S(1)} custom-call(s32[5,128]{1,0:T(8,128)S(1)} %get-tuple-element.48.tables_ref, s32[200]{0:T(256)S(1)} %get-tuple-element.49.reader_ref, s32[200]{0:T(256)S(1)} %get-tuple-element.50.key_ref, s32[192]{0:T(256)S(1)} %get-tuple-element.51.slot_ref, bf16[64,64,256]{2,1,0:T(8,128)(2,1)} %get-tuple-element.52.blocks_ref, ...), custom_call_target="tpu_custom_call" | custom-call | tf_op jit(solution)/shard_map/cond/branch_1_fun/pallas_call | solution.py:729
  131.5 5.1 %shard_map.83 = bf16[4096,256]{1,0:T(8,128)(2,1)} custom-call(bf16[4096,256]{1,0:T(8,128)(2,1)} %get-tuple-element.60.placed_ref, bf16[4096,256]{1,0:T(8,128)(2,1)S(1)} %get-tuple-element.148.attended_ref, bf16[256,256]{1,0:T(8,128)(2,1)} %wo_ref.1, bf16[256,256]{1,0:T(8,128)(2,1)} %wm_ref.1), custom_call_target="tpu_custom_call" | custom-call | tf_op jit(solution)/shard_map/pallas_call | solution.py:737
  (35 shorter events, 0.5 us)
Async XLA Ops:
  0.0 18.5 %copy-start.2 = (bf16[256,256]{1,0:T(8,128)(2,1)S(1)}, bf16[256,256]{1,0:T(8,128)(2,1)}, u32[]{:S(2)}) copy-start(bf16[256,256]{1,0:T(8,128)(2,1)} %param.15) | copy-start | bytes 393220
  0.0 18.6 %copy-start.1 = (bf16[256,256]{1,0:T(8,128)(2,1)S(1)}, bf16[256,256]{1,0:T(8,128)(2,1)}, u32[]{:S(2)}) copy-start(bf16[256,256]{1,0:T(8,128)(2,1)} %param.14) | copy-start | bytes 393220
  0.0 18.6 %copy-start = (bf16[256,256]{1,0:T(8,128)(2,1)S(1)}, bf16[256,256]{1,0:T(8,128)(2,1)}, u32[]{:S(2)}) copy-start(bf16[256,256]{1,0:T(8,128)(2,1)} %param.13) | copy-start | bytes 393220

commit v7 on v6

--- a/solution.py
+++ b/solution.py
@@ -652,7 +652,7 @@
     batch = math.gcd(groups, 2)
     tile = pl.BlockSpec((batch * group_rows, width), lambda i: (i, 0))
     full = (2 * capacity, 2 * capacity, block_count, block_count)
-    small = (capacity + 18, capacity + 18, capacity + 27, capacity + 34)
+    small = (capacity + 17, capacity + 17, capacity + 27, capacity + 33)
     limits = tuple(min(a, b) for a, b in zip(small, full))
     teams = lax.axis_size("groups") * stride
     placed, normed, needs, over = pl.pallas_call(

time: 137 us -> 136 us (level)
  no operation moved by 1% of the time
where the time goes in v7:
time: 136 us
  Pallas kernels  129 us (95%)
  local copies, waits for them, and re-layouts  2.73 us (2%)
  other arithmetic  2.4 us (2%)
    pallas_call x1, Pallas kernels, body(): lax.cond(over[0, 0] <= 0.0, layer(0, limits), layer(2, full), tables, rea...  112 us
    pallas_call x1, Pallas kernels, body(): pl.pallas_call(functools.partial(place_kernel, stride, limits), grid=(gro...  12.2 us
    pallas_call x1, Pallas kernels, body(): pl.pallas_call(finish_kernel, grid=(rows_dev // finish_rows,), in_specs=[...  5.12 us

profile of v7, /device:TPU:12, one launch (start us, length us, event | category | flops | bytes accessed | tf_op | source)
XLA Modules:
  0.0 135.9 jit_solution(11719773134729836687)
XLA Ops:
  0.0 0.0 copy-start.2
  0.0 0.0 copy-start.1
  0.0 0.0 copy-start
  0.2 0.1 broadcast_in_dim.180
  0.3 0.1 broadcast_in_dim.181
  0.4 0.1 broadcast_in_dim.176
  0.4 0.1 broadcast_in_dim.177
  0.5 0.1 broadcast_in_dim.174
  0.6 0.1 broadcast_in_dim.175
  0.7 0.1 broadcast_in_dim.179
  0.7 0.8 copy.10
  1.5 0.1 reshape.1667
  1.7 0.7 select_reduce_fusion.1
  2.4 12.2 %shard_map.82 = (bf16[4096,256]{1,0:T(8,128)(2,1)}, bf16[4096,256]{1,0:T(8,128)(2,1)}, s32[8,4,128]{2,1,0:T(4,128)}, f32[1,1]{1,0:T(1,128)}) custom-call(s32[8,1,512]{2,1,0:T(1,128)} %bitcast.71, s32[4,128]{1,0:T(4,128)} %bitcast.74, bf16[4096,256]{1,0:T(8,128)(2,1)} %features_ref.1), custom_call_target="tpu_custom_call" | custom-call | tf_op jit(solution)/shard_map/pallas_call | solution.py:658
  15.2 0.8 reshape_reshape.3
  16.2 0.1 convolution_convert_fusion
  16.3 0.1 squeeze.21
  16.4 0.1 select_reduce_fusion.8
  16.6 0.1 fusion.17
  16.8 0.1 fusion.5
  16.9 0.1 constant_dynamic-update-slice_fusion.3
  17.0 0.2 reduce_sum.112
  17.2 0.1 fusion.2
  17.4 0.1 broadcast_select_fusion
  17.5 0.1 select_n.295
  17.5 0.2 select_reduce_fusion
  17.7 0.1 select_reduce_fusion.5
  17.8 0.1 select_reduce_fusion.4
  18.0 0.1 select_reduce_fusion.6
  18.1 0.1 select_reduce_fusion.7
  18.2 0.2 select_reduce_fusion.3
  18.4 0.1 select_reduce_fusion.2
  18.5 0.0 copy-done.2
  18.6 0.0 copy-done.1
  18.6 0.0 copy-done
  18.6 112.2 %conditional.1 = (bf16[4096,256]{1,0:T(8,128)(2,1)S(1)}) conditional(s32[]{:T(128)} %bitcast.2, (s32[5,128]{1,0:T(8,128)S(1)}, s32[200]{0:T(256)S(1)}, s32[200]{0:T(256)S(1)}, s32[192]{0:T(256)S(1)}, bf16[64,64,256]{2,1,0:T(8,128)(2,1)}, /*index=5*/bf16[256,256]{1,0:T(8,128)(2,1)S(1)}, bf16[256,256]{1,0:T(8,128)(2,1)S(1)}, ...), branch_computations={%region_15.16_spmd, %region_16.17_spmd} | conditional | bytes 8 | solution.py:729
  18.8 111.7 %branch_1_fun.1 = bf16[4096,256]{1,0:T(8,128)(2,1)S(1)} custom-call(s32[5,128]{1,0:T(8,128)S(1)} %get-tuple-element.48.tables_ref, s32[200]{0:T(256)S(1)} %get-tuple-element.49.reader_ref, s32[200]{0:T(256)S(1)} %get-tuple-element.50.key_ref, s32[192]{0:T(256)S(1)} %get-tuple-element.51.slot_ref, bf16[64,64,256]{2,1,0:T(8,128)(2,1)} %get-tuple-element.52.blocks_ref, ...), custom_call_target="tpu_custom_call" | custom-call | tf_op jit(solution)/shard_map/cond/branch_1_fun/pallas_call | solution.py:729
  130.8 5.1 %shard_map.83 = bf16[4096,256]{1,0:T(8,128)(2,1)} custom-call(bf16[4096,256]{1,0:T(8,128)(2,1)} %get-tuple-element.60.placed_ref, bf16[4096,256]{1,0:T(8,128)(2,1)S(1)} %get-tuple-element.148.attended_ref, bf16[256,256]{1,0:T(8,128)(2,1)} %wo_ref.1, bf16[256,256]{1,0:T(8,128)(2,1)} %wm_ref.1), custom_call_target="tpu_custom_call" | custom-call | tf_op jit(solution)/shard_map/pallas_call | solution.py:737
  (35 shorter events, 0.5 us)
Async XLA Ops:
  0.0 18.5 %copy-start.2 = (bf16[256,256]{1,0:T(8,128)(2,1)S(1)}, bf16[256,256]{1,0:T(8,128)(2,1)}, u32[]{:S(2)}) copy-start(bf16[256,256]{1,0:T(8,128)(2,1)} %param.15) | copy-start | bytes 393220
  0.0 18.6 %copy-start.1 = (bf16[256,256]{1,0:T(8,128)(2,1)S(1)}, bf16[256,256]{1,0:T(8,128)(2,1)}, u32[]{:S(2)}) copy-start(bf16[256,256]{1,0:T(8,128)(2,1)} %param.14) | copy-start | bytes 393220
  0.0 18.6 %copy-start = (bf16[256,256]{1,0:T(8,128)(2,1)S(1)}, bf16[256,256]{1,0:T(8,128)(2,1)}, u32[]{:S(2)}) copy-start(bf16[256,256]{1,0:T(8,128)(2,1)} %param.13) | copy-start | bytes 393220

commit v8 on v7

--- a/solution.py
+++ b/solution.py
@@ -277,7 +277,7 @@
     far, late, side = [far0, far1], [rest0, rest1], [side0, side1]
     near_limit, end_limit, first_limit, union_limit = limits
     part_one = (cap + 1) // 2
-    part_two = cap + (end_limit - cap + 1) // 2
+    part_two = cap + 2 * (end_limit - cap) // 3
     bounds = [0, part_one, cap, part_two, end_limit]
     relayed = len(bounds) - 1
     for bound in (first_limit, union_limit):

time: 136 us -> 136 us (level)
  no operation moved by 1% of the time
where the time goes in v8:
time: 136 us
  Pallas kernels  129 us (95%)
  local copies, waits for them, and re-layouts  2.73 us (2%)
  other arithmetic  2.4 us (2%)
    pallas_call x1, Pallas kernels, body(): lax.cond(over[0, 0] <= 0.0, layer(0, limits), layer(2, full), tables, rea...  112 us
    pallas_call x1, Pallas kernels, body(): pl.pallas_call(functools.partial(place_kernel, stride, limits), grid=(gro...  12.2 us
    pallas_call x1, Pallas kernels, body(): pl.pallas_call(finish_kernel, grid=(rows_dev // finish_rows,), in_specs=[...  5.12 us

profile of v8, /device:TPU:12, one launch (start us, length us, event | category | flops | bytes accessed | tf_op | source)
XLA Modules:
  0.0 135.9 jit_solution(1223779909294181990)
XLA Ops:
  0.0 0.0 copy-start.2
  0.0 0.0 copy-start.1
  0.0 0.0 copy-start
  0.2 0.1 broadcast_in_dim.180
  0.3 0.1 broadcast_in_dim.181
  0.4 0.1 broadcast_in_dim.176
  0.4 0.1 broadcast_in_dim.177
  0.5 0.1 broadcast_in_dim.174
  0.6 0.1 broadcast_in_dim.175
  0.7 0.1 broadcast_in_dim.179
  0.7 0.8 copy.10
  1.5 0.1 reshape.1667
  1.7 0.7 select_reduce_fusion.1
  2.4 12.2 %shard_map.82 = (bf16[4096,256]{1,0:T(8,128)(2,1)}, bf16[4096,256]{1,0:T(8,128)(2,1)}, s32[8,4,128]{2,1,0:T(4,128)}, f32[1,1]{1,0:T(1,128)}) custom-call(s32[8,1,512]{2,1,0:T(1,128)} %bitcast.71, s32[4,128]{1,0:T(4,128)} %bitcast.74, bf16[4096,256]{1,0:T(8,128)(2,1)} %features_ref.1), custom_call_target="tpu_custom_call" | custom-call | tf_op jit(solution)/shard_map/pallas_call | solution.py:658
  15.2 0.8 reshape_reshape.3
  16.2 0.1 convolution_convert_fusion
  16.3 0.1 squeeze.21
  16.4 0.1 select_reduce_fusion.8
  16.6 0.1 fusion.17
  16.8 0.1 fusion.5
  16.9 0.1 constant_dynamic-update-slice_fusion.3
  17.0 0.2 reduce_sum.112
  17.2 0.1 fusion.2
  17.4 0.1 broadcast_select_fusion
  17.5 0.1 select_n.295
  17.5 0.2 select_reduce_fusion
  17.7 0.1 select_reduce_fusion.5
  17.8 0.1 select_reduce_fusion.4
  18.0 0.1 select_reduce_fusion.6
  18.1 0.1 select_reduce_fusion.7
  18.2 0.2 select_reduce_fusion.3
  18.4 0.1 select_reduce_fusion.2
  18.5 0.0 copy-done.2
  18.6 0.0 copy-done.1
  18.6 0.0 copy-done
  18.6 112.2 %conditional.1 = (bf16[4096,256]{1,0:T(8,128)(2,1)S(1)}) conditional(s32[]{:T(128)} %bitcast.2, (s32[5,128]{1,0:T(8,128)S(1)}, s32[200]{0:T(256)S(1)}, s32[200]{0:T(256)S(1)}, s32[192]{0:T(256)S(1)}, bf16[64,64,256]{2,1,0:T(8,128)(2,1)}, /*index=5*/bf16[256,256]{1,0:T(8,128)(2,1)S(1)}, bf16[256,256]{1,0:T(8,128)(2,1)S(1)}, ...), branch_computations={%region_15.16_spmd, %region_16.17_spmd} | conditional | bytes 8 | solution.py:729
  18.8 111.7 %branch_1_fun.1 = bf16[4096,256]{1,0:T(8,128)(2,1)S(1)} custom-call(s32[5,128]{1,0:T(8,128)S(1)} %get-tuple-element.48.tables_ref, s32[200]{0:T(256)S(1)} %get-tuple-element.49.reader_ref, s32[200]{0:T(256)S(1)} %get-tuple-element.50.key_ref, s32[192]{0:T(256)S(1)} %get-tuple-element.51.slot_ref, bf16[64,64,256]{2,1,0:T(8,128)(2,1)} %get-tuple-element.52.blocks_ref, ...), custom_call_target="tpu_custom_call" | custom-call | tf_op jit(solution)/shard_map/cond/branch_1_fun/pallas_call | solution.py:729
  130.8 5.1 %shard_map.83 = bf16[4096,256]{1,0:T(8,128)(2,1)} custom-call(bf16[4096,256]{1,0:T(8,128)(2,1)} %get-tuple-element.60.placed_ref, bf16[4096,256]{1,0:T(8,128)(2,1)S(1)} %get-tuple-element.148.attended_ref, bf16[256,256]{1,0:T(8,128)(2,1)} %wo_ref.1, bf16[256,256]{1,0:T(8,128)(2,1)} %wm_ref.1), custom_call_target="tpu_custom_call" | custom-call | tf_op jit(solution)/shard_map/pallas_call | solution.py:737
  (35 shorter events, 0.5 us)
Async XLA Ops:
  0.0 18.5 %copy-start.2 = (bf16[256,256]{1,0:T(8,128)(2,1)S(1)}, bf16[256,256]{1,0:T(8,128)(2,1)}, u32[]{:S(2)}) copy-start(bf16[256,256]{1,0:T(8,128)(2,1)} %param.15) | copy-start | bytes 393220
  0.0 18.6 %copy-start.1 = (bf16[256,256]{1,0:T(8,128)(2,1)S(1)}, bf16[256,256]{1,0:T(8,128)(2,1)}, u32[]{:S(2)}) copy-start(bf16[256,256]{1,0:T(8,128)(2,1)} %param.14) | copy-start | bytes 393220
  0.0 18.6 %copy-start = (bf16[256,256]{1,0:T(8,128)(2,1)S(1)}, bf16[256,256]{1,0:T(8,128)(2,1)}, u32[]{:S(2)}) copy-start(bf16[256,256]{1,0:T(8,128)(2,1)} %param.13) | copy-start | bytes 393220
